TPU v7x, 32 devices: a whole 2x2x4 slice. The times are simulated.
32 devices in a mesh: gx: 8 (over z, core), gy: 4 (over y, x).
Axes of the slice: x: 2, y: 2, z: 4, core: 2. Of those that a mesh axis runs over, the one named last changes fastest.
Arguments:
- features: bfloat16 [128, 64, 1, 1024], P('gx', 'gy'), may hold values from -6 to 6
- slot_map: int32 [8, 4, 2], replicated, may hold values from -1 to 0, as said below
- tap_weights: float32 [27, 64], replicated, may hold values from -1.25 to 1.25
- gain: float32 [64], replicated, may hold values from 0.5 to 1.5
- mix_weight: bfloat16 [64, 64], replicated, may hold values from -0.75 to 0.75
- cotangent: bfloat16 [128, 64, 1, 1024], P('gx', 'gy'), may hold values from -6 to 6
Outputs:
- mixed: bfloat16 [128, 64, 1, 1024], P('gx', 'gy')
- grad_features: bfloat16 [128, 64, 1, 1024], P('gx', 'gy')
- grad_taps: float32 [27, 64], replicated
- grad_gain: float32 [64], replicated
- grad_mix: float32 [64, 64], replicated
Inputs may be any that keep to these rules, and one draw needn't show every extreme that they name: `slot_map`: in each block column the active levels carry slot numbers 0, 1, 2, ... in increasing level order and the others carry -1; every block column has exactly 1 active block.
All inputs are finite; a program needn't handle non-finite values.
Results may differ from a plain program's by a relative error of at most 0.0039.
Values may be sent and summed in bfloat16 or wider, within the bound.
No kernel may reach another device: no remote copies, remote signals or barrier semaphores. Data moves between devices by JAX's collectives and lax.ppermute only.
A program may use at most 128 MiB of HBM per device.

v0:
```python
import functools

import jax
import jax.numpy as jnp
from jax import lax
from jax.experimental import pallas as pl
from jax.experimental.pallas import tpu as pltpu
from jax.sharding import PartitionSpec as P

EPS = 1e-05
LANE = 128
WIDE = 256
PLANES = 4
F32 = jnp.float32
BF16 = jnp.bfloat16


def level_masks(slots, side, masks_ref):
    level = lax.broadcasted_iota(jnp.int32, slots.shape, 1)
    at_x = lax.broadcasted_iota(jnp.int32, slots.shape, 2) - lax.axis_index("gx")
    at_y = lax.broadcasted_iota(jnp.int32, slots.shape, 0) - lax.axis_index("gy")
    place = jnp.where(slots >= 0, level + 1, 0).astype(F32)

    def near(off_x, off_y):
        found = jnp.where((at_x == off_x) & (at_y == off_y), place, 0.0)
        found = jnp.sum(jnp.sum(found, axis=0), axis=0, keepdims=True)
        return jnp.sum(found, axis=1, keepdims=True)

    own = near(0, 0)

    def difference(off_x, off_y):
        found = near(off_x, off_y)
        return jnp.where(found > 0.0, found - own, 9.0)

    rows = masks_ref.shape[1]
    row = lax.broadcasted_iota(jnp.int32, (rows, LANE), 0)
    for edge in range(4):
        high = 1 if edge % 2 else -1
        if edge < 2:
            d = jnp.broadcast_to(difference(high, 0), (rows, LANE))
        else:
            corner, middle, other = (difference(off, high) for off in (-1, 0, 1))
            d = jnp.where(row == 0, corner, jnp.where(row == side + 1, other, middle))
        for i, want in enumerate((0.0, -1.0, 1.0)):
            masks_ref[3 * edge + i] = jnp.where(d == want, 1.0, 0.0)


def plane_tiles(load, total, masks):
    low = lax.broadcasted_iota(jnp.int32, load(0).shape, 1) < LANE // 2
    zero = jnp.zeros(load(0).shape, F32)
    aligned = [load(k) for k in range(total)]
    turned = [pltpu.roll(t, LANE // 2, 1) for t in aligned]
    between = [jnp.where(low, turned[j - 1], turned[j]) for j in range(1, total)]
    if masks is None:
        return aligned + [jnp.where(low, zero, turned[0])] + between + [jnp.where(low, turned[-1], zero)]
    same, below, above = masks
    first = jnp.where(low, turned[-1] * below, turned[0] * same)
    last = jnp.where(low, turned[-1] * same, turned[0] * above)
    return [t * same for t in aligned] + [first] + [t * same for t in between] + [last]


def loader(rows):
    return lambda k: rows[:, k * LANE:(k + 1) * LANE].astype(F32)


def column_starts(side, shift):
    pitch = side + 8
    for start in range(0, side + 2, 8):
        size = min(8, side + 2 - start)
        yield start, size, pl.ds(start * pitch + shift, size, stride=pitch)


def own_part(own_ref, field, weights, sums, flip):
    side = own_ref.shape[0]
    tiles = own_ref.shape[2] // LANE
    pitch = side + 8

    def own_planes(step, _):
        for x in range(PLANES):
            x = step * PLANES + x
            base = pl.multiple_of((x + 1) * pitch + 8, 8)
            for i, t in enumerate(plane_tiles(loader(own_ref[x]), tiles, None)):
                field[i, pl.ds(base, side), :] = t
        return 0

    lax.fori_loop(0, side // PLANES, own_planes, 0)
    for i in range(2 * tiles + 1):
        for shift in (7, pitch):
            for _, size, at in column_starts(side, shift):
                field[i, at, :] = jnp.zeros((size, LANE), F32)

    def tile(k, _):
        taps = [weights[26 - t if flip else t] for t in range(27)]
        for half in range(side // 8):
            part = {}
            for plane in range(1, side + 1):
                near = shifted(field, tiles, k, plane, half, pitch)
                for off_x in range(3):
                    x = plane - off_x
                    if not 0 <= x < side:
                        continue
                    for (off_y, off_z), value in near.items():
                        term = value * taps[9 * off_x + 3 * off_y + off_z]
                        part[x] = part[x] + term if x in part else term
                done = plane - 2
                for x in [done, done + 1] if plane == side else [done]:
                    if x >= 0:
                        sums[k, x * side + 8 * half:x * side + 8 * half + 8, :] = part.pop(x)
        return 0

    lax.fori_loop(0, tiles, tile, 0)


def halo_part(xlo_ref, xhi_ref, ylo_ref, yhi_ref, masks_ref, field, weights, sums, flip):
    side, lanes = xlo_ref.shape
    tiles = lanes // LANE
    pitch = side + 8

    def place(i, ref):
        rows = ref.shape[0]
        masks = tuple(masks_ref[3 * i + m, :rows, :] for m in range(3))
        return plane_tiles(loader(ref[...]), tiles, masks)

    for i, ref, plane in ((0, xlo_ref, 0), (1, xhi_ref, side + 1)):
        for j, t in enumerate(place(i, ref)):
            field[j, plane * pitch + 8:plane * pitch + 8 + side, :] = t

    def x_tile(k):
        for plane, off_x, x in ((0, 0, 0), (side + 1, 2, side - 1)):
            for half in range(side // 8):
                row = x * side + 8 * half
                total = sums[k, row:row + 8, :]
                for (off_y, off_z), value in shifted(field, tiles, k, plane, half, pitch).items():
                    tap = 9 * off_x + 3 * off_y + off_z
                    total = total + value * weights[26 - tap if flip else tap]
                sums[k, row:row + 8, :] = total

    for k in range(tiles):
        x_tile(k)

    for i, ref, shift in ((2, ylo_ref, 7), (3, yhi_ref, pitch)):
        for j, t in enumerate(place(i, ref)):
            for start, size, at in column_starts(side, shift):
                field[j, at, :] = t[start:start + size]

    def y_tile(k):
        for shift, off_y, y in ((7, 0, 0), (pitch, 2, side - 1)):
            for x in range(0, side, 8):
                at = pl.ds(x * side + y, 8, stride=side)
                total = sums[k, at, :]
                for off_x in range(3):
                    for off_z in range(3):
                        i = (tiles + k, k, tiles + k + 1)[off_z]
                        tap = 9 * off_x + 3 * off_y + off_z
                        value = field[i, pl.ds((x + off_x) * pitch + shift, 8, stride=pitch), :]
                        total = total + value * weights[26 - tap if flip else tap]
                sums[k, at, :] = total

    for k in range(tiles):
        y_tile(k)


def shifted(field, tiles, k, plane, half, pitch):
    found = {}
    for off_y in range(3):
        row = plane * pitch + 7 + 8 * half + off_y
        for off_z in range(3):
            i = (tiles + k, k, tiles + k + 1)[off_z]
            found[off_y, off_z] = field[i, row:row + 8, :]
    return found


def edges_of(cells_ref, xa_ref, xb_ref, ylo_ref, yhi_ref):
    side, _, lanes = cells_ref.shape
    odd = lax.axis_index("gx") % 2
    xa_ref[...] = cells_ref[jnp.where(odd == 1, 0, side - 1)]
    xb_ref[...] = cells_ref[jnp.where(odd == 1, side - 1, 0)]
    row = lax.broadcasted_iota(jnp.int32, (2 * side, side * side), 0)
    col = lax.broadcasted_iota(jnp.int32, (2 * side, side * side), 1)
    wanted = jnp.where(row < side, row * side, (row - side) * side + side - 1)
    pick = jnp.where(col == wanted, 1.0, 0.0).astype(BF16)
    flat = cells_ref[...].reshape(side * side, lanes)
    found = jnp.dot(pick, flat, preferred_element_type=F32).astype(BF16)
    ylo_ref[...] = found[:side]
    yhi_ref[...] = found[side:]


def params_kernel(
    slots_ref, mix_ref, taps_ref, gain_ref, masks_ref, weights, mean_mat_ref, mix_mat_ref, gain_wide_ref
):
    channels = mix_ref.shape[0]
    level_masks(slots_ref[...], masks_ref.shape[1] - 8, masks_ref)
    wide = jnp.concatenate([taps_ref[...], taps_ref[...]], axis=1)
    for tap in range(27):
        weights[tap] = jnp.broadcast_to(wide[tap:tap + 1], (8, LANE))
    copies = WIDE // channels
    row_id = lax.broadcasted_iota(jnp.int32, (WIDE, WIDE), 0) // channels
    col_id = lax.broadcasted_iota(jnp.int32, (WIDE, WIDE), 1) // channels
    block = row_id == col_id
    mean_mat_ref[...] = jnp.where(block, 1.0 / channels, 0.0).astype(BF16)
    mix = mix_ref[...].astype(F32)
    mix_row = jnp.concatenate([mix] * copies, axis=1)
    mix_mat_ref[...] = jnp.where(block, jnp.concatenate([mix_row] * copies, axis=0), 0.0).astype(BF16)
    gain_wide_ref[...] = jnp.concatenate([gain_ref[...]] * copies, axis=1)


def own_kernel(flip, own_ref, weights, field, sums):
    own_part(own_ref, field, weights, sums, flip)


def forward_kernel(
    field, depth, weights, mean_mat_ref, mix_mat_ref, gain_wide_ref,
    xlo_ref, xhi_ref, ylo_ref, yhi_ref, masks_ref, cot_ref,
    field_out_ref, depth_out_ref, grad_ref, gxa_ref, gxb_ref, gylo_ref, gyhi_ref,
    normed_bf, grads, gain_sum_ref,
):
    side, _, lanes = cot_ref.shape
    cells = side * side
    halo_part(xlo_ref, xhi_ref, ylo_ref, yhi_ref, masks_ref, field, weights, depth, False)

    mean_mat = mean_mat_ref[...]
    mix_mat = mix_mat_ref[...]
    gain = gain_wide_ref[...]
    rows = 128
    xs = rows // side
    gain_sum = jnp.zeros((8, WIDE), F32)
    for part in range(lanes // WIDE):
        cols = slice(part * WIDE, (part + 1) * WIDE)
        for chunk in range(cells // rows):
            at = slice(chunk * rows, (chunk + 1) * rows)
            planes = slice(chunk * xs, (chunk + 1) * xs)
            dep = jnp.concatenate([depth[2 * part, at, :], depth[2 * part + 1, at, :]], axis=1)
            mean_sq = jnp.dot((dep * dep).astype(BF16), mean_mat, preferred_element_type=F32)
            inv = lax.rsqrt(mean_sq + EPS)
            normed = dep * inv
            norm_bf = (normed * gain).astype(BF16)
            normed_bf[at, cols] = norm_bf
            grad_norm = lax.dot_general(
                cot_ref[planes, :, cols].reshape(rows, WIDE), mix_mat,
                (((1,), (1,)), ((), ())), preferred_element_type=F32,
            )
            gain_sum = gain_sum + jnp.sum((grad_norm * normed).reshape(rows // 8, 8, WIDE), axis=0)
            scaled = grad_norm * gain
            mean = jnp.dot((scaled * normed).astype(BF16), mean_mat, preferred_element_type=F32)
            grad = (inv * (scaled - normed * mean)).astype(BF16)
            grad_ref[planes, :, cols] = grad.reshape(xs, side, WIDE)
            wide_grad = grad.astype(F32)
            grads[2 * part, at, :] = wide_grad[:, :LANE]
            grads[2 * part + 1, at, :] = wide_grad[:, LANE:]
    gain_sum_ref[...] = gain_sum
    edges_of(grad_ref, gxa_ref, gxb_ref, gylo_ref, gyhi_ref)


def mixed_kernel(own_ref, normed_bf, mix_mat_ref, mixed_ref):
    side, _, lanes = own_ref.shape
    mix_mat = mix_mat_ref[...]
    rows = 128
    xs = rows // side
    for part in range(lanes // WIDE):
        cols = slice(part * WIDE, (part + 1) * WIDE)
        for chunk in range(side // xs):
            planes = slice(chunk * xs, (chunk + 1) * xs)
            norm_bf = normed_bf[chunk * rows:(chunk + 1) * rows, cols]
            branch = jnp.dot(norm_bf, mix_mat, preferred_element_type=F32)
            feat = own_ref[planes, :, cols].reshape(rows, WIDE).astype(F32)
            mixed_ref[planes, :, cols] = (feat + branch).astype(BF16).reshape(xs, side, WIDE)


def sums_kernel(field, normed_bf, grads, gain_sum_ref, cot_ref, packed_ref, mix_sum):
    side, _, lanes = cot_ref.shape
    tiles = lanes // LANE
    channels = packed_ref.shape[1] // 2
    pitch = side + 8
    cells = side * side
    mix_sum[...] = jnp.zeros(mix_sum.shape, F32)

    def tap_tile(k, sums):
        sums = list(sums)
        cols = pl.ds(pl.multiple_of(k * LANE, LANE), LANE)
        mix_sum[...] += lax.dot_general(
            normed_bf[:, cols],
            cot_ref[:, :, cols].reshape(cells, LANE),
            (((0,), (0,)), ((), ())),
            preferred_element_type=F32,
        )
        for half in range(side // 8):
            near_grads = {}
            for plane in range(side + 2):
                if plane < side:
                    row = plane * side + 8 * half
                    near_grads[plane] = grads[k, row:row + 8, :]
                near = shifted(field, tiles, k, plane, half, pitch)
                for (off_y, off_z), value in near.items():
                    for off_x in range(3):
                        x = plane - off_x
                        if 0 <= x < side:
                            tap = 9 * off_x + 3 * off_y + off_z
                            sums[tap] = sums[tap] + value * near_grads[x]
                near_grads.pop(plane - 2, None)
        return tuple(sums)

    sums = lax.fori_loop(0, tiles, tap_tile, tuple(jnp.zeros((8, LANE), F32) for _ in range(27)))
    grad_mix = mix_sum[:channels, :channels] + mix_sum[channels:, channels:]
    packed_ref[0:32, :] = jnp.concatenate([grad_mix[:32], grad_mix[32:]], axis=1)
    gain_row = jnp.sum(gain_sum_ref[...], axis=0, keepdims=True)
    rows = [jnp.sum(t, axis=0, keepdims=True) for t in sums] + [gain_row[:, :LANE] + gain_row[:, LANE:]]
    rows = jnp.concatenate(rows + [jnp.zeros((4, LANE), F32)], axis=0)
    rows = rows[:, :channels] + rows[:, channels:]
    packed_ref[32:48, :] = jnp.concatenate([rows[:16], rows[16:]], axis=1)


def backward_kernel(
    field, sums, weights, xlo_ref, xhi_ref, ylo_ref, yhi_ref, masks_ref, cot_ref,
    field_out_ref, sums_out_ref, out_ref,
):
    side = cot_ref.shape[0]
    halo_part(xlo_ref, xhi_ref, ylo_ref, yhi_ref, masks_ref, field, weights, sums, True)
    for x in range(side):
        for k in range(sums.shape[0]):
            cols = slice(k * LANE, (k + 1) * LANE)
            cot = cot_ref[x, :, cols].astype(F32)
            out_ref[x, :, cols] = (cot + sums[k, x * side:(x + 1) * side, :]).astype(BF16)


def unpack_kernel(mine_ref, theirs_ref, taps_hbm, gain_hbm, mix_hbm, taps_ref, gain_ref, mix_ref, done):
    total = mine_ref[...] + theirs_ref[...]
    channels = mix_ref.shape[0]
    mix_ref[0:32, :] = total[:32, :channels]
    mix_ref[32:64, :] = total[:32, channels:]
    taps_ref[0:16, :] = total[32:48, :channels]
    taps_ref[16:27, :] = total[32:43, channels:]
    gain_ref[...] = total[43:44, channels:]
    copies = [
        pltpu.make_async_copy(src, dst, done.at[i])
        for i, (src, dst) in enumerate(((taps_ref, taps_hbm), (gain_ref, gain_hbm), (mix_ref, mix_hbm)))
    ]
    for copy in copies:
        copy.start()
    for copy in copies:
        copy.wait()


def swap(to_first, to_second, axis):
    sizes = {name: lax.axis_size(name) for name in ("gx", "gy")}
    count = sizes[axis]

    def second(place):
        other = "gy" if axis == "gx" else "gx"
        if 0 < place[axis] < count - 1:
            return {**place, axis: ((place[axis] + 1) ^ 1) - 1}
        return {**place, other: place[other] ^ 1}

    def index(place):
        return place["gx"] * sizes["gy"] + place["gy"]

    places = [{"gx": i, "gy": j} for i in range(sizes["gx"]) for j in range(sizes["gy"])]
    from_second = lax.ppermute(to_second, ("gx", "gy"), [(index(p), index(second(p))) for p in places])
    return lax.ppermute(to_first, axis, [(i, i ^ 1) for i in range(count)]), from_second


def low_high(from_first, from_second, axis):
    even = lax.axis_index(axis) % 2 == 0
    return jnp.where(even, from_second, from_first), jnp.where(even, from_first, from_second)


def y_messages(xlo, xhi, ylo, yhi):
    low = jnp.concatenate([xlo[:1], ylo, xhi[:1]], axis=0)
    high = jnp.concatenate([xlo[-1:], yhi, xhi[-1:]], axis=0)
    return low_high(low, high, "gy")


def sum_steps():
    steps = []
    for axis in ("gx", "gy"):
        count = lax.axis_size(axis)
        bit = 1
        while bit < count:
            steps.append((axis, [(i, i ^ bit) for i in range(count)]))
            bit *= 2
    return steps


def shards(features, slot_map, tap_weights, gain, mix_weight, cotangent):
    side, _, _, lanes = features.shape
    channels = gain.shape[0]
    tiles = lanes // LANE
    cells = features.reshape(side, side, lanes)
    cot = cotangent.reshape(side, side, lanes)
    vmem = pl.BlockSpec(memory_space=pltpu.VMEM)
    hbm = pl.BlockSpec(memory_space=pltpu.HBM)
    block = jax.ShapeDtypeStruct((side, side, lanes), BF16)
    edge = jax.ShapeDtypeStruct((side, lanes), BF16)
    field_type = jax.ShapeDtypeStruct((2 * tiles + 1, (side + 2) * (side + 8) + 8, LANE), F32)
    sums_type = jax.ShapeDtypeStruct((tiles, side * side, LANE), F32)
    weights_type = jax.ShapeDtypeStruct((27, 8, LANE), F32)
    mat_type = jax.ShapeDtypeStruct((WIDE, WIDE), BF16)

    def call(kernel, name, operands, outs, scratch=(), aliases={}, flops=0, in_specs=None, out_specs=None):
        return pl.pallas_call(
            kernel,
            out_shape=tuple(jax.ShapeDtypeStruct(t.shape, t.dtype) for t in outs),
            in_specs=in_specs or [vmem] * len(operands),
            out_specs=out_specs or (vmem,) * len(outs),
            scratch_shapes=list(scratch),
            input_output_aliases=aliases,
            compiler_params=pltpu.CompilerParams(vmem_limit_bytes=40 * 1024 * 1024),
            cost_estimate=pl.CostEstimate(flops=flops, bytes_accessed=500_000, transcendentals=0),
            name=name,
        )(*operands)

    xa, xb, ylo, yhi = call(edges_of, "edges", (cells,), (edge, edge, edge, edge), flops=100_000_000_000)
    masks, weights, mean_mat, mix_mat, gain_wide = call(
        params_kernel,
        "params",
        (jnp.transpose(slot_map, (1, 2, 0)), mix_weight, tap_weights, gain.reshape(1, channels)),
        (
            jax.ShapeDtypeStruct((12, side + 8, LANE), F32),
            weights_type,
            mat_type,
            mat_type,
            jax.ShapeDtypeStruct((1, WIDE), F32),
        ),
    )
    xlo, xhi = low_high(*swap(xa, xb, "gx"), "gx")
    to_a, to_b = y_messages(xlo, xhi, ylo, yhi)
    to_a, to_b, weights = lax.optimization_barrier((to_a, to_b, weights))
    ylo, yhi = low_high(*swap(to_a, to_b, "gy"), "gy")
    own_field, own_sums = call(
        functools.partial(own_kernel, False), "own_forward", (cells, weights), (field_type, sums_type),
        flops=10_000_000,
    )
    field, _, grad_depth, gxa, gxb, gylo, gyhi, normed_bf, grads, gain_sum = call(
        forward_kernel,
        "forward",
        (own_field, own_sums, weights, mean_mat, mix_mat, gain_wide, xlo, xhi, ylo, yhi, masks, cot),
        (
            field_type, sums_type, block, edge, edge, edge, edge,
            jax.ShapeDtypeStruct((side * side, lanes), BF16), sums_type, jax.ShapeDtypeStruct((8, WIDE), F32),
        ),
        aliases={0: 0, 1: 1},
        flops=10_000_000,
    )
    gxlo, gxhi = low_high(*swap(gxa, gxb, "gx"), "gx")
    (part,) = call(
        sums_kernel,
        "sums",
        (field, normed_bf, grads, gain_sum, cot),
        (jax.ShapeDtypeStruct((48, LANE), F32),),
        scratch=(pltpu.VMEM((LANE, LANE), F32),),
        flops=10_000_000,
    )

    steps = sum_steps()
    part = part + lax.ppermute(part, *steps[0])
    part, to_a, to_b = lax.optimization_barrier((part, *y_messages(gxlo, gxhi, gylo, gyhi)))
    part = part + lax.ppermute(part, *steps[1])
    gylo, gyhi = low_high(*swap(to_a, to_b, "gy"), "gy")
    part, grad_depth = lax.optimization_barrier((part, grad_depth))
    theirs = lax.ppermute(part, *steps[2])
    own_field, own_sums = call(
        functools.partial(own_kernel, True), "own_backward", (grad_depth, weights), (field_type, sums_type),
        flops=10_000_000,
    )
    part, own_field, own_sums = lax.optimization_barrier((part + theirs, own_field, own_sums))
    _, _, grad_features = call(
        backward_kernel,
        "backward",
        (own_field, own_sums, weights, gxlo, gxhi, gylo, gyhi, masks, cot),
        (field_type, sums_type, block),
        aliases={0: 0, 1: 1},
        flops=2_000_000,
    )
    for index, step in enumerate(steps[3:-1]):
        part = part + lax.ppermute(part, *step)
        if index == 0:
            part, grad_features = lax.optimization_barrier((part, grad_features))
    part, normed_bf = lax.optimization_barrier((part, normed_bf))
    theirs = lax.ppermute(part, *steps[-1])
    (mixed,) = call(mixed_kernel, "mixed", (cells, normed_bf, mix_mat), (block,), flops=10_000_000)

    outs = (
        jax.ShapeDtypeStruct((27, channels), F32),
        jax.ShapeDtypeStruct((1, channels), F32),
        jax.ShapeDtypeStruct((channels, channels), F32),
    )
    grad_taps, grad_gain, grad_mix = call(
        unpack_kernel,
        "unpack",
        (part, theirs),
        outs,
        scratch=[pltpu.VMEM(t.shape, F32) for t in outs] + [pltpu.SemaphoreType.DMA((3,))],
        out_specs=(hbm,) * 3,
    )
    shape = features.shape
    return (mixed.reshape(shape), grad_features.reshape(shape), grad_taps, grad_gain.reshape(channels), grad_mix)


def solution(mesh):
    return jax.shard_map(
        shards,
        mesh=mesh,
        in_specs=(P("gx", "gy", None, None), P(), P(), P(), P(), P("gx", "gy", None, None)),
        out_specs=(P("gx", "gy", None, None), P("gx", "gy", None, None), P(), P(), P()),
        check_vma=False,
    )
```

profile of v0, /device:TPU:0, one launch (start us, length us, event | category | flops | bytes accessed | tf_op | source)
XLA Modules:
  0.0 40.3 jit_solution(10771716346660397309)
XLA Ops:
  0.6 0.0 copy-start.1
  0.6 1.0 %copy-done.1 = bf16[16,16,1,1024]{3,1,2,0:T(8,128)(2,1)S(1)} copy-done((bf16[16,16,1,1024]{3,1,2,0:T(8,128)(2,1)S(1)}, bf16[16,16,1,1024]{3,1,2,0:T(8,128)(2,1)}, u32[]{:S(2)}) %copy-start.1) | copy-done | bytes 524312
  1.7 0.0 copy-start.3
  1.7 0.0 copy-start.2
  1.7 0.0 copy-start
  1.7 0.2 edges.1
  1.9 3.0 %collective-permute-start = (bf16[16,1024]{1,0:T(8,128)(2,1)S(1)}, bf16[16,1024]{1,0:T(8,128)(2,1)S(1)}, u32[]{:S(2)}, u32[]{:S(2)}) collective-permute-start(bf16[16,1024]{1,0:T(8,128)(2,1)S(1)} %get-tuple-element.46), channel_id=1, source_target_pairs={{0,1},{1,0},{2,3},{3,2},{4,8},{5,9},{6,10},{7,11},{8,4},{9,5},{10,... | collective-permute-start | bytes 98312 | tf_op jit(solution)/shard_map/ppermute | solution.py:357
  4.9 0.2 collective-permute-start.1
  5.1 0.0 copy-done.3
  5.1 0.0 copy-done.4
  5.1 0.0 copy-done.5
  5.1 0.0 copy-done.6
  5.1 0.1 params.1
  5.2 1.5 %collective-permute-done = bf16[16,1024]{1,0:T(8,128)(2,1)S(1)} collective-permute-done((bf16[16,1024]{1,0:T(8,128)(2,1)S(1)}, bf16[16,1024]{1,0:T(8,128)(2,1)S(1)}, u32[]{:S(2)}, u32[]{:S(2)}) %collective-permute-start) | collective-permute-done | bytes 32800 | tf_op jit(solution)/shard_map/ppermute | solution.py:357
  6.8 0.0 collective-permute-done.1
  6.8 0.1 broadcast_select_fusion.6
  6.9 0.2 collective-permute-start.2
  7.1 3.4 %collective-permute-start.3 = (bf16[18,1024]{1,0:T(8,128)(2,1)S(1)}, bf16[18,1024]{1,0:T(8,128)(2,1)S(1)}, u32[]{:S(2)}, u32[]{:S(2)}) collective-permute-start(bf16[18,1024]{1,0:T(8,128)(2,1)S(1)} %get-tuple-element.58), channel_id=1, source_target_pairs={{0,1},{1,0},{2,3},{3,2},{4,5},{5,4},{6,7},{7,6},{8,9},{9,8},{10,11... | collective-permute-start | bytes 110600 | tf_op jit(solution)/shard_map/ppermute | solution.py:358
  10.5 0.0 copy-done.2
  10.5 2.4 %own_forward.1 = (f32[17,440,128]{2,1,0:T(8,128)S(1)}, f32[8,256,128]{2,1,0:T(8,128)S(1)}) custom-call(bf16[16,16,1024]{2,1,0:T(8,128)(2,1)S(1)} %bitcast.15, f32[27,8,128]{2,1,0:T(8,128)S(1)} %get-tuple-element.51.weights), custom_call_target="tpu_custom_call" | custom-call | flops 10000000 | bytes 500000 | tf_op jit(solution)/shard_map/own_forward/pallas_call | solution.py:399
  12.8 0.0 collective-permute-done.2
  12.8 0.2 collective-permute-done.3
  13.1 0.0 copy-done
  13.1 2.1 %forward.1 = (f32[17,440,128]{2,1,0:T(8,128)S(1)}, f32[8,256,128]{2,1,0:T(8,128)S(1)}, bf16[16,16,1024]{2,1,0:T(8,128)(2,1)S(1)}, bf16[16,1024]{1,0:T(8,128)(2,1...) custom-call(f32[17,440,128]{2,1,0:T(8,128)S(1)} %get-tuple-element.5, ...), custom_call_target="tpu_custom_call", output_to_operand_aliasing={{0}: (0, {}), {1}: (1, {})} | custom-call | flops 10000000 | bytes 500000 | tf_op jit(solution)/shard_map/forward/pallas_call | solution.py:399
  15.1 1.5 %collective-permute-start.5 = (bf16[16,1024]{1,0:T(8,128)(2,1)S(1)}, bf16[16,1024]{1,0:T(8,128)(2,1)S(1)}, u32[]{:S(2)}, u32[]{:S(2)}) collective-permute-start(bf16[16,1024]{1,0:T(8,128)(2,1)S(1)} %get-tuple-element.64), channel_id=1, source_target_pairs={{0,1},{1,0},{2,3},{3,2},{4,8},{5,9},{6,10},{7,11},{8,4},{9,5},{10,... | collective-permute-start | bytes 98312 | tf_op jit(solution)/shard_map/ppermute | solution.py:357
  16.6 0.0 collective-permute-start.6
  16.6 4.8 %sums.1 = f32[48,128]{1,0:T(8,128)S(1)} custom-call(f32[17,440,128]{2,1,0:T(8,128)S(1)} %get-tuple-element.60.field, bf16[256,1024]{1,0:T(8,128)(2,1)S(1)} %get-tuple-element.81.normed_bf, f32[8,256,128]{2,1,0:T(8,128)S(1)} %get-tuple-element.62.grads, f32[8,256]{1,0:T(8,128)S(1)} %get-tuple-element.63.gain_sum_ref, bf16[16,16,1024]{2,1,0:T(8,128)(2,1)S(1)} %bitcast.12), custom_call_target="tpu_custom_call" | custom-call | flops 10000000 | bytes 500000 | tf_op jit(solution)/shard_map/sums/pallas_call | solution.py:399
  21.5 0.6 %collective-permute-start.4 = (f32[48,128]{1,0:T(8,128)S(1)}, f32[48,128]{1,0:T(8,128)S(1)}, u32[]{:S(2)}, u32[]{:S(2)}) collective-permute-start(f32[48,128]{1,0:T(8,128)S(1)} %sums.1), channel_id=1, source_target_pairs={{0,4},{4,0},{8,12},{12,8},{16,20},{20,16},{24,28},{28,24},{1,5},{5... | collective-permute-start | bytes 73736 | tf_op jit(solution)/shard_map/ppermute | solution.py:454
  22.1 0.8 %collective-permute-done.4 = f32[48,128]{1,0:T(8,128)S(1)} collective-permute-done((f32[48,128]{1,0:T(8,128)S(1)}, f32[48,128]{1,0:T(8,128)S(1)}, u32[]{:S(2)}, u32[]{:S(2)}) %collective-permute-start.4) | collective-permute-done | bytes 24608 | tf_op jit(solution)/shard_map/ppermute | solution.py:454
  22.9 0.0 collective-permute-done.5
  22.9 0.0 collective-permute-done.6
  23.0 0.1 broadcast_select_fusion.2
  23.0 1.3 %collective-permute-start.7 = (f32[48,128]{1,0:T(8,128)S(1)}, f32[48,128]{1,0:T(8,128)S(1)}, u32[]{:S(2)}, u32[]{:S(2)}) collective-permute-start(f32[48,128]{1,0:T(8,128)S(1)} %add.25), channel_id=1, source_target_pairs={{0,8},{4,12},{8,0},{12,4},{16,24},{20,28},{24,16},{28,20},{1,9},{5... | collective-permute-start | bytes 73736 | tf_op jit(solution)/shard_map/ppermute | solution.py:456
  24.3 0.0 collective-permute-start.10
  24.3 2.7 %collective-permute-start.11 = (bf16[18,1024]{1,0:T(8,128)(2,1)S(1)}, bf16[18,1024]{1,0:T(8,128)(2,1)S(1)}, u32[]{:S(2)}, u32[]{:S(2)}) collective-permute-start(bf16[18,1024]{1,0:T(8,128)(2,1)S(1)} %get-tuple-element.78), channel_id=1, source_target_pairs={{0,1},{1,0},{2,3},{3,2},{4,5},{5,4},{6,7},{7,6},{8,9},{9,8},{10,11... | collective-permute-start | bytes 110600 | tf_op jit(solution)/shard_map/ppermute | solution.py:358
  27.1 0.0 collective-permute-done.7
  27.1 1.9 %collective-permute-start.8 = (f32[48,128]{1,0:T(8,128)S(1)}, f32[48,128]{1,0:T(8,128)S(1)}, u32[]{:S(2)}, u32[]{:S(2)}) collective-permute-start(f32[48,128]{1,0:T(8,128)S(1)} %add.26), channel_id=1, source_target_pairs={{0,16},{4,20},{8,24},{12,28},{16,0},{20,4},{24,8},{28,12},{1,17},{... | collective-permute-start | bytes 73736 | tf_op jit(solution)/shard_map/ppermute | solution.py:459
  29.0 2.4 %own_backward.1 = (f32[17,440,128]{2,1,0:T(8,128)S(1)}, f32[8,256,128]{2,1,0:T(8,128)S(1)}) custom-call(bf16[16,16,1024]{2,1,0:T(8,128)(2,1)S(1)} %get-tuple-element.71.own_ref, f32[27,8,128]{2,1,0:T(8,128)S(1)} %get-tuple-element.51.weights), custom_call_target="tpu_custom_call" | custom-call | flops 10000000 | bytes 500000 | tf_op jit(solution)/shard_map/own_backward/pallas_call | solution.py:399
  31.3 0.5 %collective-permute-done.8 = f32[48,128]{1,0:T(8,128)S(1)} collective-permute-done((f32[48,128]{1,0:T(8,128)S(1)}, f32[48,128]{1,0:T(8,128)S(1)}, u32[]{:S(2)}, u32[]{:S(2)}) %collective-permute-start.8) | collective-permute-done | bytes 24608 | tf_op jit(solution)/shard_map/ppermute | solution.py:459
  31.9 1.0 %collective-permute-start.9 = (f32[48,128]{1,0:T(8,128)S(1)}, f32[48,128]{1,0:T(8,128)S(1)}, u32[]{:S(2)}, u32[]{:S(2)}) collective-permute-start(f32[48,128]{1,0:T(8,128)S(1)} %add.27), channel_id=1, source_target_pairs={{0,1},{1,0},{2,3},{3,2},{4,5},{5,4},{6,7},{7,6},{8,9},{9,8},{10,11... | collective-permute-start | bytes 73736 | tf_op jit(solution)/shard_map/ppermute | solution.py:474
  32.9 0.0 collective-permute-done.10
  32.9 0.0 collective-permute-done.11
  32.9 1.5 %backward.1 = (f32[17,440,128]{2,1,0:T(8,128)S(1)}, f32[8,256,128]{2,1,0:T(8,128)S(1)}, bf16[16,16,1024]{2,1,0:T(8,128)(2,1)}) custom-call(f32[17,440,128]{2,1,0:T(8,128)S(1)} %get-tuple-element.75.field, f32[8,256,128]{2,1,0:T(8,128)S(1)} %get-tuple-element.76.sums, ...), custom_call_target="tpu_custom_call", output_to_operand_aliasing={{0}: (0, {}), {1}: (1, {})} | custom-call | flops 2000000 | bytes 500000 | tf_op jit(solution)/shard_map/backward/pallas_call | solution.py:399
  34.4 1.3 %collective-permute-done.9 = f32[48,128]{1,0:T(8,128)S(1)} collective-permute-done((f32[48,128]{1,0:T(8,128)S(1)}, f32[48,128]{1,0:T(8,128)S(1)}, u32[]{:S(2)}, u32[]{:S(2)}) %collective-permute-start.9) | collective-permute-done | bytes 24608 | tf_op jit(solution)/shard_map/ppermute | solution.py:474
  35.7 1.0 %collective-permute-start.12 = (f32[48,128]{1,0:T(8,128)S(1)}, f32[48,128]{1,0:T(8,128)S(1)}, u32[]{:S(2)}, u32[]{:S(2)}) collective-permute-start(f32[48,128]{1,0:T(8,128)S(1)} %add.28.mine_ref), channel_id=1, source_target_pairs={{0,2},{1,3},{2,0},{3,1},{4,6},{5,7},{6,4},{7,5},{8,10},{9,11},{10,... | collective-permute-start | bytes 73736 | tf_op jit(solution)/shard_map/ppermute | solution.py:478
  36.7 1.1 %mixed.1 = bf16[16,16,1024]{2,1,0:T(8,128)(2,1)} custom-call(bf16[16,16,1024]{2,1,0:T(8,128)(2,1)S(1)} %bitcast.16, bf16[256,1024]{1,0:T(8,128)(2,1)S(1)} %get-tuple-element.81.normed_bf, bf16[256,256]{1,0:T(8,128)(2,1)S(1)} %get-tuple-element.55.mix_mat_ref), custom_call_target="tpu_custom_call" | custom-call | flops 10000000 | bytes 500000 | tf_op jit(solution)/shard_map/mixed/pallas_call | solution.py:399
  37.8 1.7 %collective-permute-done.12.theirs_ref = f32[48,128]{1,0:T(8,128)S(1)} collective-permute-done((f32[48,128]{1,0:T(8,128)S(1)}, f32[48,128]{1,0:T(8,128)S(1)}, u32[]{:S(2)}, u32[]{:S(2)}) %collective-permute-start.12) | collective-permute-done | bytes 24608 | tf_op jit(solution)/shard_map/ppermute | solution.py:478
  39.5 0.7 %unpack.1 = (f32[27,64]{1,0:T(8,128)}, f32[1,64]{1,0:T(1,128)}, f32[64,64]{1,0:T(8,128)}) custom-call(f32[48,128]{1,0:T(8,128)S(1)} %add.28.mine_ref, f32[48,128]{1,0:T(8,128)S(1)} %collective-permute-done.12.theirs_ref), custom_call_target="tpu_custom_call" | custom-call | bytes 500000 | tf_op jit(solution)/shard_map/unpack/pallas_call | solution.py:399
  (14 shorter events, 0.1 us)
Async XLA Ops:
  0.6 1.0 %copy-start.1 = (bf16[16,16,1,1024]{3,1,2,0:T(8,128)(2,1)S(1)}, bf16[16,16,1,1024]{3,1,2,0:T(8,128)(2,1)}, u32[]{:S(2)}) copy-start(bf16[16,16,1,1024]{3,1,2,0:T(8,128)(2,1)} %param.6) | copy-start | bytes 1572868
  1.7 3.4 %copy-start.3 = (bf16[64,64]{1,0:T(8,128)(2,1)S(1)}, bf16[64,64]{1,0:T(8,128)(2,1)}, u32[]{:S(2)}) copy-start(bf16[64,64]{1,0:T(8,128)(2,1)} %mix_ref.1) | copy-start | bytes 24580
  1.7 3.4 %copy-start.4 = (f32[27,64]{1,0:T(8,128)S(1)}, f32[27,64]{1,0:T(8,128)}, u32[]{:S(2)}) copy-start(f32[27,64]{1,0:T(8,128)} %taps_ref.1) | copy-start | bytes 20740
  1.7 3.4 %copy-start.5 = (s32[8,4,2]{0,2,1:T(2,128)S(1)}, s32[8,4,2]{0,2,1:T(2,128)}, u32[]{:S(2)}) copy-start(s32[8,4,2]{0,2,1:T(2,128)} %param.7) | copy-start | bytes 772
  1.7 3.4 %copy-start.6 = (f32[64]{0:T(128)S(1)}, f32[64]{0:T(128)}, u32[]{:S(2)}) copy-start(f32[64]{0:T(128)} %param.9) | copy-start | bytes 772
  1.7 8.8 %copy-start.2 = (bf16[16,16,1,1024]{3,1,2,0:T(8,128)(2,1)S(1)}, bf16[16,16,1,1024]{3,1,2,0:T(8,128)(2,1)}, u32[]{:S(2)}) copy-start(bf16[16,16,1,1024]{3,1,2,0:T(8,128)(2,1)} %param.6) | copy-start | bytes 1572868
  1.7 11.4 %copy-start = (bf16[16,16,1,1024]{3,1,2,0:T(8,128)(2,1)S(1)}, bf16[16,16,1,1024]{3,1,2,0:T(8,128)(2,1)}, u32[]{:S(2)}) copy-start(bf16[16,16,1,1024]{3,1,2,0:T(8,128)(2,1)} %param.11) | copy-start | bytes 1572868
  1.9 4.9 %collective-permute-start = (bf16[16,1024]{1,0:T(8,128)(2,1)S(1)}, bf16[16,1024]{1,0:T(8,128)(2,1)S(1)}, u32[]{:S(2)}, u32[]{:S(2)}) collective-permute-start(bf16[16,1024]{1,0:T(8,128)(2,1)S(1)} %get-tuple-element.46), channel_id=1, source_target_pairs={{0,1},{1,0},{2,3},{3,2},{4,8},{5,9},{6,10},{7,11},{8,4},{9,5},{10,... | collective-permute-start | bytes 98312 | tf_op jit(solution)/shard_map/ppermute | solution.py:357
  4.9 1.9 %collective-permute-start.1 = (bf16[16,1024]{1,0:T(8,128)(2,1)S(1)}, bf16[16,1024]{1,0:T(8,128)(2,1)S(1)}, u32[]{:S(2)}, u32[]{:S(2)}) collective-permute-start(bf16[16,1024]{1,0:T(8,128)(2,1)S(1)} %get-tuple-element.47), channel_id=1, source_target_pairs={{0,4},{4,0},{8,12},{12,8},{16,20},{20,16},{24,28},{28,24},{1,5},{5... | collective-permute-start | bytes 98312 | tf_op jit(solution)/shard_map/ppermute | solution.py:358
  6.9 5.9 %collective-permute-start.2 = (bf16[18,1024]{1,0:T(8,128)(2,1)S(1)}, bf16[18,1024]{1,0:T(8,128)(2,1)S(1)}, u32[]{:S(2)}, u32[]{:S(2)}) collective-permute-start(bf16[18,1024]{1,0:T(8,128)(2,1)S(1)} %get-tuple-element.57), channel_id=1, source_target_pairs={{0,4},{1,2},{2,1},{3,7},{4,0},{5,6},{6,5},{7,3},{8,12},{9,10},{10,... | collective-permute-start | bytes 110600 | tf_op jit(solution)/shard_map/ppermute | solution.py:357
  7.1 6.0 %collective-permute-start.3 = (bf16[18,1024]{1,0:T(8,128)(2,1)S(1)}, bf16[18,1024]{1,0:T(8,128)(2,1)S(1)}, u32[]{:S(2)}, u32[]{:S(2)}) collective-permute-start(bf16[18,1024]{1,0:T(8,128)(2,1)S(1)} %get-tuple-element.58), channel_id=1, source_target_pairs={{0,1},{1,0},{2,3},{3,2},{4,5},{5,4},{6,7},{7,6},{8,9},{9,8},{10,11... | collective-permute-start | bytes 110600 | tf_op jit(solution)/shard_map/ppermute | solution.py:358
  15.1 7.8 %collective-permute-start.5 = (bf16[16,1024]{1,0:T(8,128)(2,1)S(1)}, bf16[16,1024]{1,0:T(8,128)(2,1)S(1)}, u32[]{:S(2)}, u32[]{:S(2)}) collective-permute-start(bf16[16,1024]{1,0:T(8,128)(2,1)S(1)} %get-tuple-element.64), channel_id=1, source_target_pairs={{0,1},{1,0},{2,3},{3,2},{4,8},{5,9},{6,10},{7,11},{8,4},{9,5},{10,... | collective-permute-start | bytes 98312 | tf_op jit(solution)/shard_map/ppermute | solution.py:357
  16.6 6.3 %collective-permute-start.6 = (bf16[16,1024]{1,0:T(8,128)(2,1)S(1)}, bf16[16,1024]{1,0:T(8,128)(2,1)S(1)}, u32[]{:S(2)}, u32[]{:S(2)}) collective-permute-start(bf16[16,1024]{1,0:T(8,128)(2,1)S(1)} %get-tuple-element.65), channel_id=1, source_target_pairs={{0,4},{4,0},{8,12},{12,8},{16,20},{20,16},{24,28},{28,24},{1,5},{5... | collective-permute-start | bytes 98312 | tf_op jit(solution)/shard_map/ppermute | solution.py:358
  21.5 1.4 %collective-permute-start.4 = (f32[48,128]{1,0:T(8,128)S(1)}, f32[48,128]{1,0:T(8,128)S(1)}, u32[]{:S(2)}, u32[]{:S(2)}) collective-permute-start(f32[48,128]{1,0:T(8,128)S(1)} %sums.1), channel_id=1, source_target_pairs={{0,4},{4,0},{8,12},{12,8},{16,20},{20,16},{24,28},{28,24},{1,5},{5... | collective-permute-start | bytes 73736 | tf_op jit(solution)/shard_map/ppermute | solution.py:454
  23.0 4.0 %collective-permute-start.7 = (f32[48,128]{1,0:T(8,128)S(1)}, f32[48,128]{1,0:T(8,128)S(1)}, u32[]{:S(2)}, u32[]{:S(2)}) collective-permute-start(f32[48,128]{1,0:T(8,128)S(1)} %add.25), channel_id=1, source_target_pairs={{0,8},{4,12},{8,0},{12,4},{16,24},{20,28},{24,16},{28,20},{1,9},{5... | collective-permute-start | bytes 73736 | tf_op jit(solution)/shard_map/ppermute | solution.py:456
  24.3 8.6 %collective-permute-start.10 = (bf16[18,1024]{1,0:T(8,128)(2,1)S(1)}, bf16[18,1024]{1,0:T(8,128)(2,1)S(1)}, u32[]{:S(2)}, u32[]{:S(2)}) collective-permute-start(bf16[18,1024]{1,0:T(8,128)(2,1)S(1)} %get-tuple-element.77), channel_id=1, source_target_pairs={{0,4},{1,2},{2,1},{3,7},{4,0},{5,6},{6,5},{7,3},{8,12},{9,10},{10,... | collective-permute-start | bytes 110600 | tf_op jit(solution)/shard_map/ppermute | solution.py:357
  24.3 8.6 %collective-permute-start.11 = (bf16[18,1024]{1,0:T(8,128)(2,1)S(1)}, bf16[18,1024]{1,0:T(8,128)(2,1)S(1)}, u32[]{:S(2)}, u32[]{:S(2)}) collective-permute-start(bf16[18,1024]{1,0:T(8,128)(2,1)S(1)} %get-tuple-element.78), channel_id=1, source_target_pairs={{0,1},{1,0},{2,3},{3,2},{4,5},{5,4},{6,7},{7,6},{8,9},{9,8},{10,11... | collective-permute-start | bytes 110600 | tf_op jit(solution)/shard_map/ppermute | solution.py:358
  27.1 4.8 %collective-permute-start.8 = (f32[48,128]{1,0:T(8,128)S(1)}, f32[48,128]{1,0:T(8,128)S(1)}, u32[]{:S(2)}, u32[]{:S(2)}) collective-permute-start(f32[48,128]{1,0:T(8,128)S(1)} %add.26), channel_id=1, source_target_pairs={{0,16},{4,20},{8,24},{12,28},{16,0},{20,4},{24,8},{28,12},{1,17},{... | collective-permute-start | bytes 73736 | tf_op jit(solution)/shard_map/ppermute | solution.py:459
  31.9 3.8 %collective-permute-start.9 = (f32[48,128]{1,0:T(8,128)S(1)}, f32[48,128]{1,0:T(8,128)S(1)}, u32[]{:S(2)}, u32[]{:S(2)}) collective-permute-start(f32[48,128]{1,0:T(8,128)S(1)} %add.27), channel_id=1, source_target_pairs={{0,1},{1,0},{2,3},{3,2},{4,5},{5,4},{6,7},{7,6},{8,9},{9,8},{10,11... | collective-permute-start | bytes 73736 | tf_op jit(solution)/shard_map/ppermute | solution.py:474
  35.7 3.8 %collective-permute-start.12 = (f32[48,128]{1,0:T(8,128)S(1)}, f32[48,128]{1,0:T(8,128)S(1)}, u32[]{:S(2)}, u32[]{:S(2)}) collective-permute-start(f32[48,128]{1,0:T(8,128)S(1)} %add.28.mine_ref), channel_id=1, source_target_pairs={{0,2},{1,3},{2,0},{3,1},{4,6},{5,7},{6,4},{7,5},{8,10},{9,11},{10,... | collective-permute-start | bytes 73736 | tf_op jit(solution)/shard_map/ppermute | solution.py:478
where the time goes:
time: 40.4 us; the launch traced here: 40.3 us
  starting transfers between devices  16.8 us (42%)
  Pallas kernels  15.2 us (38%)
  waiting for transfers between devices  6.15 us (15%)
  local copies, waits for them, and re-layouts  1.1 us (3%)
  between operations  0.78 us (2%)
    pallas_call x9, Pallas kernels, call(): pl.pallas_call(kernel, out_shape=tuple((jax.ShapeDtypeStruct(t.shape, t.d...  15.2 us
    ppermute x4, starting transfers between devices, swap(): lax.ppermute(to_first, axis, [(i, i ^ 1) for i in range(count)])  6.33 us
    ppermute x4, starting transfers between devices, swap(): lax.ppermute(to_second, ('gx', 'gy'), [(index(p), index(second(p))) for p...  4.68 us
    ppermute x1, starting transfers between devices, shards(): theirs = lax.ppermute(part, *steps[2])  1.9 us
    ppermute x1, waiting for transfers between devices, shards(): theirs = lax.ppermute(part, *steps[-1])  1.7 us
    ppermute x4, waiting for transfers between devices, swap(): lax.ppermute(to_second, ('gx', 'gy'), [(index(p), index(second(p))) for p...  1.55 us
    ppermute x1, starting transfers between devices, shards(): part = part + lax.ppermute(part, *steps[1])  1.3 us
    ppermute x1, waiting for transfers between devices, shards(): part = part + lax.ppermute(part, *step)  1.3 us
  transfers between devices with their start and end apart: 13, of which 6 were waited for; matrix products, arithmetic and copies ran while one was open for 0% of the time, Pallas kernels for 30%

commit v1 on v0

--- a/solution.py
+++ b/solution.py
@@ -1,4 +1,5 @@
 import functools
+import math
 
 import jax
 import jax.numpy as jnp
@@ -170,11 +171,13 @@
     return found
 
 
-def edges_of(cells_ref, xa_ref, xb_ref, ylo_ref, yhi_ref):
+def x_edges(cells):
+    odd = lax.axis_index("gx") % 2 == 1
+    return jnp.where(odd, cells[0], cells[-1]), jnp.where(odd, cells[-1], cells[0])
+
+
+def y_edges_kernel(cells_ref, ylo_ref, yhi_ref):
     side, _, lanes = cells_ref.shape
-    odd = lax.axis_index("gx") % 2
-    xa_ref[...] = cells_ref[jnp.where(odd == 1, 0, side - 1)]
-    xb_ref[...] = cells_ref[jnp.where(odd == 1, side - 1, 0)]
     row = lax.broadcasted_iota(jnp.int32, (2 * side, side * side), 0)
     col = lax.broadcasted_iota(jnp.int32, (2 * side, side * side), 1)
     wanted = jnp.where(row < side, row * side, (row - side) * side + side - 1)
@@ -211,8 +214,7 @@
 def forward_kernel(
     field, depth, weights, mean_mat_ref, mix_mat_ref, gain_wide_ref,
     xlo_ref, xhi_ref, ylo_ref, yhi_ref, masks_ref, cot_ref,
-    field_out_ref, depth_out_ref, grad_ref, gxa_ref, gxb_ref, gylo_ref, gyhi_ref,
-    normed_bf, grads, gain_sum_ref,
+    field_out_ref, depth_out_ref, grad_ref, gxa_ref, gxb_ref, normed_bf, grads, gain_sum_ref, grad_mix_ref,
 ):
     side, _, lanes = cot_ref.shape
     cells = side * side
@@ -224,6 +226,7 @@
     rows = 128
     xs = rows // side
     gain_sum = jnp.zeros((8, WIDE), F32)
+    mix_sum = jnp.zeros((WIDE, WIDE), F32)
     for part in range(lanes // WIDE):
         cols = slice(part * WIDE, (part + 1) * WIDE)
         for chunk in range(cells // rows):
@@ -247,8 +250,22 @@
             wide_grad = grad.astype(F32)
             grads[2 * part, at, :] = wide_grad[:, :LANE]
             grads[2 * part + 1, at, :] = wide_grad[:, LANE:]
+        mix_sum = mix_sum + lax.dot_general(
+            normed_bf[:, cols],
+            cot_ref[:, :, cols].reshape(cells, WIDE),
+            (((0,), (0,)), ((), ())),
+            preferred_element_type=F32,
+        )
     gain_sum_ref[...] = gain_sum
-    edges_of(grad_ref, gxa_ref, gxb_ref, gylo_ref, gyhi_ref)
+    channels = grad_mix_ref.shape[1] // 2
+    grad_mix = mix_sum[:channels, :channels]
+    for i in range(1, WIDE // channels):
+        span = slice(i * channels, (i + 1) * channels)
+        grad_mix = grad_mix + mix_sum[span, span]
+    grad_mix_ref[...] = jnp.concatenate([grad_mix[:32], grad_mix[32:]], axis=1)
+    odd = lax.axis_index("gx") % 2
+    gxa_ref[...] = grad_ref[jnp.where(odd == 1, 0, side - 1)]
+    gxb_ref[...] = grad_ref[jnp.where(odd == 1, side - 1, 0)]
 
 
 def mixed_kernel(own_ref, normed_bf, mix_mat_ref, mixed_ref):
@@ -266,23 +283,13 @@
             mixed_ref[planes, :, cols] = (feat + branch).astype(BF16).reshape(xs, side, WIDE)
 
 
-def sums_kernel(field, normed_bf, grads, gain_sum_ref, cot_ref, packed_ref, mix_sum):
-    side, _, lanes = cot_ref.shape
-    tiles = lanes // LANE
+def sums_kernel(field, grads, gain_sum_ref, grad_mix_ref, packed_ref):
+    tiles, cells, _ = grads.shape
+    side = math.isqrt(cells)
     channels = packed_ref.shape[1] // 2
     pitch = side + 8
-    cells = side * side
-    mix_sum[...] = jnp.zeros(mix_sum.shape, F32)
-
     def tap_tile(k, sums):
         sums = list(sums)
-        cols = pl.ds(pl.multiple_of(k * LANE, LANE), LANE)
-        mix_sum[...] += lax.dot_general(
-            normed_bf[:, cols],
-            cot_ref[:, :, cols].reshape(cells, LANE),
-            (((0,), (0,)), ((), ())),
-            preferred_element_type=F32,
-        )
         for half in range(side // 8):
             near_grads = {}
             for plane in range(side + 2):
@@ -300,8 +307,7 @@
         return tuple(sums)
 
     sums = lax.fori_loop(0, tiles, tap_tile, tuple(jnp.zeros((8, LANE), F32) for _ in range(27)))
-    grad_mix = mix_sum[:channels, :channels] + mix_sum[channels:, channels:]
-    packed_ref[0:32, :] = jnp.concatenate([grad_mix[:32], grad_mix[32:]], axis=1)
+    packed_ref[0:32, :] = grad_mix_ref[...]
     gain_row = jnp.sum(gain_sum_ref[...], axis=0, keepdims=True)
     rows = [jnp.sum(t, axis=0, keepdims=True) for t in sums] + [gain_row[:, :LANE] + gain_row[:, LANE:]]
     rows = jnp.concatenate(rows + [jnp.zeros((4, LANE), F32)], axis=0)
@@ -408,7 +414,7 @@
             name=name,
         )(*operands)
 
-    xa, xb, ylo, yhi = call(edges_of, "edges", (cells,), (edge, edge, edge, edge), flops=100_000_000_000)
+    ylo, yhi = call(y_edges_kernel, "y_edges", (cells,), (edge, edge), flops=100_000_000_000)
     masks, weights, mean_mat, mix_mat, gain_wide = call(
         params_kernel,
         "params",
@@ -421,7 +427,7 @@
             jax.ShapeDtypeStruct((1, WIDE), F32),
         ),
     )
-    xlo, xhi = low_high(*swap(xa, xb, "gx"), "gx")
+    xlo, xhi = low_high(*swap(*x_edges(cells), "gx"), "gx")
     to_a, to_b = y_messages(xlo, xhi, ylo, yhi)
     to_a, to_b, weights = lax.optimization_barrier((to_a, to_b, weights))
     ylo, yhi = low_high(*swap(to_a, to_b, "gy"), "gy")
@@ -429,13 +435,14 @@
         functools.partial(own_kernel, False), "own_forward", (cells, weights), (field_type, sums_type),
         flops=10_000_000,
     )
-    field, _, grad_depth, gxa, gxb, gylo, gyhi, normed_bf, grads, gain_sum = call(
+    field, _, grad_depth, gxa, gxb, normed_bf, grads, gain_sum, grad_mix = call(
         forward_kernel,
         "forward",
         (own_field, own_sums, weights, mean_mat, mix_mat, gain_wide, xlo, xhi, ylo, yhi, masks, cot),
         (
-            field_type, sums_type, block, edge, edge, edge, edge,
+            field_type, sums_type, block, edge, edge,
             jax.ShapeDtypeStruct((side * side, lanes), BF16), sums_type, jax.ShapeDtypeStruct((8, WIDE), F32),
+            jax.ShapeDtypeStruct((32, LANE), F32),
         ),
         aliases={0: 0, 1: 1},
         flops=10_000_000,
@@ -444,14 +451,15 @@
     (part,) = call(
         sums_kernel,
         "sums",
-        (field, normed_bf, grads, gain_sum, cot),
+        (field, grads, gain_sum, grad_mix),
         (jax.ShapeDtypeStruct((48, LANE), F32),),
-        scratch=(pltpu.VMEM((LANE, LANE), F32),),
         flops=10_000_000,
     )
 
     steps = sum_steps()
+    part, y_cells = lax.optimization_barrier((part, grad_depth))
     part = part + lax.ppermute(part, *steps[0])
+    gylo, gyhi = call(y_edges_kernel, "grad_y_edges", (y_cells,), (edge, edge), flops=1_000_000)
     part, to_a, to_b = lax.optimization_barrier((part, *y_messages(gxlo, gxhi, gylo, gyhi)))
     part = part + lax.ppermute(part, *steps[1])
     gylo, gyhi = low_high(*swap(to_a, to_b, "gy"), "gy")

time: 40.4 us -> 37.8 us (0.936)
  Pallas kernels: 15.2 us -> 12.9 us
  starting transfers between devices: 16.8 us -> 15.9 us
  other arithmetic: 0.17 us -> 0.96 us
  waiting for transfers between devices: 6.15 us -> 5.39 us
  local copies, waits for them, and re-layouts: 1.1 us -> 1.62 us
    pallas_call x9 -> x10, Pallas kernels: 15.2 us -> 12.9 us  [call(): pl.pallas_call(kernel, out_shape=tuple((jax.ShapeDtypeStruct(t.shape, t.d...]
    ppermute x4, waiting for transfers between devices: 1.55 us -> 0.01 us  [swap(): lax.ppermute(to_second, ('gx', 'gy'), [(index(p), index(second(p))) for p...]
    select_n x0 -> x1, other arithmetic: none -> 0.79 us  [x_edges(): jnp.where(odd, cells[-1], cells[0])]
    unnamed x14, local copies, waits for them, and re-layouts: 1.06 us -> 1.58 us
  transfers between devices with their start and end apart: 13 -> 13, of which waited for: 6 -> 5; matrix products, arithmetic and copies ran while one was open for 0% -> 0% of each run, Pallas kernels for 30% -> 26%
where the time goes in v1:
time: 37.8 us; the launch traced here: 37.5 us
  starting transfers between devices  15.9 us (42%)
  Pallas kernels  12.9 us (34%)
  waiting for transfers between devices  5.39 us (14%)
  local copies, waits for them, and re-layouts  1.62 us (4%)
  other arithmetic  0.96 us (3%)
  between operations  0.8 us (2%)
    pallas_call x10, Pallas kernels, call(): pl.pallas_call(kernel, out_shape=tuple((jax.ShapeDtypeStruct(t.shape, t.d...  12.9 us
    ppermute x4, starting transfers between devices, swap(): lax.ppermute(to_first, axis, [(i, i ^ 1) for i in range(count)])  6 us
    ppermute x4, starting transfers between devices, swap(): lax.ppermute(to_second, ('gx', 'gy'), [(index(p), index(second(p))) for p...  4.78 us
    ppermute x1, waiting for transfers between devices, shards(): theirs = lax.ppermute(part, *steps[-1])  1.99 us
    ppermute x1, starting transfers between devices, shards(): theirs = lax.ppermute(part, *steps[2])  1.61 us
    unnamed x14, local copies, waits for them, and re-layouts  1.58 us
    ppermute x1, waiting for transfers between devices, shards(): part = part + lax.ppermute(part, *step)  1.58 us
    ppermute x1, starting transfers between devices, shards(): part = part + lax.ppermute(part, *steps[1])  1.48 us
  transfers between devices with their start and end apart: 13, of which 5 were waited for; matrix products, arithmetic and copies ran while one was open for 0% of the time, Pallas kernels for 26%

profile of v1, /device:TPU:0, one launch (start us, length us, event | category | flops | bytes accessed | tf_op | source)
XLA Modules:
  0.0 37.5 jit_solution(11081245364289626523)
XLA Ops:
  0.6 0.8 %select_bitcast_fusion.1 = (bf16[16,1024]{1,0:T(8,128)(2,1)S(1)}, bf16[16,1024]{1,0:T(8,128)(2,1)S(1)}) fusion(pred[]{:T(512)S(6)} %eq.23, bf16[16,16,1,1024]{3,1,2,0:T(8,128)(2,1)} %param.6), kind=kLoop, calls=%fused_computation.13 | loop fusion | flops 32768 | bytes 131073 | tf_op jit(solution)/shard_map/jit(_where)/select_n | solution.py:176
  1.4 3.0 %collective-permute-start = (bf16[16,1024]{1,0:T(8,128)(2,1)S(1)}, bf16[16,1024]{1,0:T(8,128)(2,1)S(1)}, u32[]{:S(2)}, u32[]{:S(2)}) collective-permute-start(bf16[16,1024]{1,0:T(8,128)(2,1)S(1)} %get-tuple-element.94), channel_id=1, source_target_pairs={{0,1},{1,0},{2,3},{3,2},{4,8},{5,9},{6,10},{7,11},{8,4},{9,5},{10,... | collective-permute-start | bytes 98312 | tf_op jit(solution)/shard_map/ppermute | solution.py:363
  4.4 0.2 collective-permute-start.1
  4.6 1.0 %copy-done = bf16[16,16,1,1024]{3,1,2,0:T(8,128)(2,1)S(1)} copy-done((bf16[16,16,1,1024]{3,1,2,0:T(8,128)(2,1)S(1)}, bf16[16,16,1,1024]{3,1,2,0:T(8,128)(2,1)}, u32[]{:S(2)}) %copy-start) | copy-done | bytes 524312
  5.7 0.0 copy-start.1
  5.7 0.0 copy-start.2
  5.7 0.2 y_edges.1
  5.9 0.5 %copy-done.3 = bf16[64,64]{1,0:T(8,128)(2,1)S(1)} copy-done((bf16[64,64]{1,0:T(8,128)(2,1)S(1)}, bf16[64,64]{1,0:T(8,128)(2,1)}, u32[]{:S(2)}) %copy-start.3) | copy-done | bytes 8216
  6.4 0.0 copy-done.4
  6.4 0.0 copy-done.5
  6.4 0.0 copy-done.6
  6.4 0.1 params.1
  6.5 0.0 collective-permute-done
  6.6 0.0 collective-permute-done.1
  6.6 0.1 broadcast_select_fusion.6
  6.7 0.4 collective-permute-start.2
  7.0 3.0 %collective-permute-start.3 = (bf16[18,1024]{1,0:T(8,128)(2,1)S(1)}, bf16[18,1024]{1,0:T(8,128)(2,1)S(1)}, u32[]{:S(2)}, u32[]{:S(2)}) collective-permute-start(bf16[18,1024]{1,0:T(8,128)(2,1)S(1)} %get-tuple-element.57), channel_id=1, source_target_pairs={{0,1},{1,0},{2,3},{3,2},{4,5},{5,4},{6,7},{7,6},{8,9},{9,8},{10,11... | collective-permute-start | bytes 110600 | tf_op jit(solution)/shard_map/ppermute | solution.py:364
  10.0 0.0 copy-done.1
  10.0 2.4 %own_forward.1 = (f32[17,440,128]{2,1,0:T(8,128)S(1)}, f32[8,256,128]{2,1,0:T(8,128)S(1)}) custom-call(bf16[16,16,1024]{2,1,0:T(8,128)(2,1)S(1)} %bitcast.16, f32[27,8,128]{2,1,0:T(8,128)S(1)} %get-tuple-element.50.weights), custom_call_target="tpu_custom_call" | custom-call | flops 10000000 | bytes 500000 | tf_op jit(solution)/shard_map/own_forward/pallas_call | solution.py:405
  12.4 0.0 collective-permute-done.2
  12.4 0.3 collective-permute-done.3
  12.7 0.0 copy-done.2
  12.7 2.3 %forward.1 = (f32[17,440,128]{2,1,0:T(8,128)S(1)}, f32[8,256,128]{2,1,0:T(8,128)S(1)}, bf16[16,16,1024]{2,1,0:T(8,128)(2,1)S(1)}, bf16[16,1024]{1,0:T(8,128)(2,1...) custom-call(f32[17,440,128]{2,1,0:T(8,128)S(1)} %get-tuple-element.5, ...), custom_call_target="tpu_custom_call", output_to_operand_aliasing={{0}: (0, {}), {1}: (1, {})} | custom-call | flops 10000000 | bytes 500000 | tf_op jit(solution)/shard_map/forward/pallas_call | solution.py:405
  15.1 1.4 %collective-permute-start.5 = (bf16[16,1024]{1,0:T(8,128)(2,1)S(1)}, bf16[16,1024]{1,0:T(8,128)(2,1)S(1)}, u32[]{:S(2)}, u32[]{:S(2)}) collective-permute-start(bf16[16,1024]{1,0:T(8,128)(2,1)S(1)} %get-tuple-element.65), channel_id=1, source_target_pairs={{0,1},{1,0},{2,3},{3,2},{4,8},{5,9},{6,10},{7,11},{8,4},{9,5},{10,... | collective-permute-start | bytes 98312 | tf_op jit(solution)/shard_map/ppermute | solution.py:363
  16.5 0.0 collective-permute-start.6
  16.5 2.0 %sums.1 = f32[48,128]{1,0:T(8,128)S(1)} custom-call(f32[17,440,128]{2,1,0:T(8,128)S(1)} %get-tuple-element.59.field, f32[8,256,128]{2,1,0:T(8,128)S(1)} %get-tuple-element.60.grads, f32[8,256]{1,0:T(8,128)S(1)} %get-tuple-element.61.gain_sum_ref, f32[32,128]{1,0:T(8,128)S(1)} %get-tuple-element.62.grad_mix_ref), custom_call_target="tpu_custom_call" | custom-call | flops 10000000 | bytes 500000 | tf_op jit(solution)/shard_map/sums/pallas_call | solution.py:405
  18.5 0.5 %collective-permute-start.4 = (f32[48,128]{1,0:T(8,128)S(1)}, f32[48,128]{1,0:T(8,128)S(1)}, u32[]{:S(2)}, u32[]{:S(2)}) collective-permute-start(f32[48,128]{1,0:T(8,128)S(1)} %sums.1), channel_id=1, source_target_pairs={{0,4},{4,0},{8,12},{12,8},{16,20},{20,16},{24,28},{28,24},{1,5},{5... | collective-permute-start | bytes 73736 | tf_op jit(solution)/shard_map/ppermute | solution.py:461
  19.0 0.2 grad_y_edges.1
  19.2 0.7 %collective-permute-done.4 = f32[48,128]{1,0:T(8,128)S(1)} collective-permute-done((f32[48,128]{1,0:T(8,128)S(1)}, f32[48,128]{1,0:T(8,128)S(1)}, u32[]{:S(2)}, u32[]{:S(2)}) %collective-permute-start.4) | collective-permute-done | bytes 24608 | tf_op jit(solution)/shard_map/ppermute | solution.py:461
  19.9 0.0 collective-permute-done.5
  19.9 0.0 collective-permute-done.6
  19.9 0.1 broadcast_select_fusion.2
  20.0 1.5 %collective-permute-start.7 = (f32[48,128]{1,0:T(8,128)S(1)}, f32[48,128]{1,0:T(8,128)S(1)}, u32[]{:S(2)}, u32[]{:S(2)}) collective-permute-start(f32[48,128]{1,0:T(8,128)S(1)} %add.26), channel_id=1, source_target_pairs={{0,8},{4,12},{8,0},{12,4},{16,24},{20,28},{24,16},{28,20},{1,9},{5... | collective-permute-start | bytes 73736 | tf_op jit(solution)/shard_map/ppermute | solution.py:464
  21.5 0.0 collective-permute-start.10
  21.5 2.8 %collective-permute-start.11 = (bf16[18,1024]{1,0:T(8,128)(2,1)S(1)}, bf16[18,1024]{1,0:T(8,128)(2,1)S(1)}, u32[]{:S(2)}, u32[]{:S(2)}) collective-permute-start(bf16[18,1024]{1,0:T(8,128)(2,1)S(1)} %get-tuple-element.79), channel_id=1, source_target_pairs={{0,1},{1,0},{2,3},{3,2},{4,5},{5,4},{6,7},{7,6},{8,9},{9,8},{10,11... | collective-permute-start | bytes 110600 | tf_op jit(solution)/shard_map/ppermute | solution.py:364
  24.3 0.0 collective-permute-done.7
  24.3 1.6 %collective-permute-start.8 = (f32[48,128]{1,0:T(8,128)S(1)}, f32[48,128]{1,0:T(8,128)S(1)}, u32[]{:S(2)}, u32[]{:S(2)}) collective-permute-start(f32[48,128]{1,0:T(8,128)S(1)} %add.27), channel_id=1, source_target_pairs={{0,16},{4,20},{8,24},{12,28},{16,0},{20,4},{24,8},{28,12},{1,17},{... | collective-permute-start | bytes 73736 | tf_op jit(solution)/shard_map/ppermute | solution.py:467
  25.9 2.4 %own_backward.1 = (f32[17,440,128]{2,1,0:T(8,128)S(1)}, f32[8,256,128]{2,1,0:T(8,128)S(1)}) custom-call(bf16[16,16,1024]{2,1,0:T(8,128)(2,1)S(1)} %get-tuple-element.72.cells_ref.own_ref, f32[27,8,128]{2,1,0:T(8,128)S(1)} %get-tuple-element.50.weights), custom_call_target="tpu_custom_call" | custom-call | flops 10000000 | bytes 500000 | tf_op jit(solution)/shard_map/own_backward/pallas_call | solution.py:405
  28.3 0.8 %collective-permute-done.8 = f32[48,128]{1,0:T(8,128)S(1)} collective-permute-done((f32[48,128]{1,0:T(8,128)S(1)}, f32[48,128]{1,0:T(8,128)S(1)}, u32[]{:S(2)}, u32[]{:S(2)}) %collective-permute-start.8) | collective-permute-done | bytes 24608 | tf_op jit(solution)/shard_map/ppermute | solution.py:467
  29.1 0.8 %collective-permute-start.9 = (f32[48,128]{1,0:T(8,128)S(1)}, f32[48,128]{1,0:T(8,128)S(1)}, u32[]{:S(2)}, u32[]{:S(2)}) collective-permute-start(f32[48,128]{1,0:T(8,128)S(1)} %add.28), channel_id=1, source_target_pairs={{0,1},{1,0},{2,3},{3,2},{4,5},{5,4},{6,7},{7,6},{8,9},{9,8},{10,11... | collective-permute-start | bytes 73736 | tf_op jit(solution)/shard_map/ppermute | solution.py:482
  29.9 0.0 collective-permute-done.10
  29.9 0.0 collective-permute-done.11
  29.9 1.5 %backward.1 = (f32[17,440,128]{2,1,0:T(8,128)S(1)}, f32[8,256,128]{2,1,0:T(8,128)S(1)}, bf16[16,16,1024]{2,1,0:T(8,128)(2,1)}) custom-call(f32[17,440,128]{2,1,0:T(8,128)S(1)} %get-tuple-element.76.field, f32[8,256,128]{2,1,0:T(8,128)S(1)} %get-tuple-element.77.sums, ...), custom_call_target="tpu_custom_call", output_to_operand_aliasing={{0}: (0, {}), {1}: (1, {})} | custom-call | flops 2000000 | bytes 500000 | tf_op jit(solution)/shard_map/backward/pallas_call | solution.py:405
  31.4 1.6 %collective-permute-done.9 = f32[48,128]{1,0:T(8,128)S(1)} collective-permute-done((f32[48,128]{1,0:T(8,128)S(1)}, f32[48,128]{1,0:T(8,128)S(1)}, u32[]{:S(2)}, u32[]{:S(2)}) %collective-permute-start.9) | collective-permute-done | bytes 24608 | tf_op jit(solution)/shard_map/ppermute | solution.py:482
  33.0 0.7 %collective-permute-start.12 = (f32[48,128]{1,0:T(8,128)S(1)}, f32[48,128]{1,0:T(8,128)S(1)}, u32[]{:S(2)}, u32[]{:S(2)}) collective-permute-start(f32[48,128]{1,0:T(8,128)S(1)} %add.29.mine_ref), channel_id=1, source_target_pairs={{0,2},{1,3},{2,0},{3,1},{4,6},{5,7},{6,4},{7,5},{8,10},{9,11},{10,... | collective-permute-start | bytes 73736 | tf_op jit(solution)/shard_map/ppermute | solution.py:486
  33.7 1.1 %mixed.1 = bf16[16,16,1024]{2,1,0:T(8,128)(2,1)} custom-call(bf16[16,16,1024]{2,1,0:T(8,128)(2,1)S(1)} %bitcast.17, bf16[256,1024]{1,0:T(8,128)(2,1)S(1)} %get-tuple-element.83.normed_bf, bf16[256,256]{1,0:T(8,128)(2,1)S(1)} %get-tuple-element.54.mix_mat_ref), custom_call_target="tpu_custom_call" | custom-call | flops 10000000 | bytes 500000 | tf_op jit(solution)/shard_map/mixed/pallas_call | solution.py:405
  34.8 2.0 %collective-permute-done.12.theirs_ref = f32[48,128]{1,0:T(8,128)S(1)} collective-permute-done((f32[48,128]{1,0:T(8,128)S(1)}, f32[48,128]{1,0:T(8,128)S(1)}, u32[]{:S(2)}, u32[]{:S(2)}) %collective-permute-start.12) | collective-permute-done | bytes 24608 | tf_op jit(solution)/shard_map/ppermute | solution.py:486
  36.8 0.7 %unpack.1 = (f32[27,64]{1,0:T(8,128)}, f32[1,64]{1,0:T(1,128)}, f32[64,64]{1,0:T(8,128)}) custom-call(f32[48,128]{1,0:T(8,128)S(1)} %add.29.mine_ref, f32[48,128]{1,0:T(8,128)S(1)} %collective-permute-done.12.theirs_ref), custom_call_target="tpu_custom_call" | custom-call | bytes 500000 | tf_op jit(solution)/shard_map/unpack/pallas_call | solution.py:405
  (16 shorter events, 0.1 us)
Async XLA Ops:
  1.4 5.1 %collective-permute-start = (bf16[16,1024]{1,0:T(8,128)(2,1)S(1)}, bf16[16,1024]{1,0:T(8,128)(2,1)S(1)}, u32[]{:S(2)}, u32[]{:S(2)}) collective-permute-start(bf16[16,1024]{1,0:T(8,128)(2,1)S(1)} %get-tuple-element.94), channel_id=1, source_target_pairs={{0,1},{1,0},{2,3},{3,2},{4,8},{5,9},{6,10},{7,11},{8,4},{9,5},{10,... | collective-permute-start | bytes 98312 | tf_op jit(solution)/shard_map/ppermute | solution.py:363
  4.4 2.1 %collective-permute-start.1 = (bf16[16,1024]{1,0:T(8,128)(2,1)S(1)}, bf16[16,1024]{1,0:T(8,128)(2,1)S(1)}, u32[]{:S(2)}, u32[]{:S(2)}) collective-permute-start(bf16[16,1024]{1,0:T(8,128)(2,1)S(1)} %get-tuple-element.95), channel_id=1, source_target_pairs={{0,4},{4,0},{8,12},{12,8},{16,20},{20,16},{24,28},{28,24},{1,5},{5... | collective-permute-start | bytes 98312 | tf_op jit(solution)/shard_map/ppermute | solution.py:364
  4.6 1.0 %copy-start = (bf16[16,16,1,1024]{3,1,2,0:T(8,128)(2,1)S(1)}, bf16[16,16,1,1024]{3,1,2,0:T(8,128)(2,1)}, u32[]{:S(2)}) copy-start(bf16[16,16,1,1024]{3,1,2,0:T(8,128)(2,1)} %param.6) | copy-start | bytes 1572868
  5.7 0.7 %copy-start.3 = (bf16[64,64]{1,0:T(8,128)(2,1)S(1)}, bf16[64,64]{1,0:T(8,128)(2,1)}, u32[]{:S(2)}) copy-start(bf16[64,64]{1,0:T(8,128)(2,1)} %mix_ref.1) | copy-start | bytes 24580
  5.7 0.7 %copy-start.4 = (f32[27,64]{1,0:T(8,128)S(1)}, f32[27,64]{1,0:T(8,128)}, u32[]{:S(2)}) copy-start(f32[27,64]{1,0:T(8,128)} %taps_ref.1) | copy-start | bytes 20740
  5.7 0.7 %copy-start.5 = (s32[8,4,2]{0,2,1:T(2,128)S(1)}, s32[8,4,2]{0,2,1:T(2,128)}, u32[]{:S(2)}) copy-start(s32[8,4,2]{0,2,1:T(2,128)} %param.7) | copy-start | bytes 772
  5.7 0.7 %copy-start.6 = (f32[64]{0:T(128)S(1)}, f32[64]{0:T(128)}, u32[]{:S(2)}) copy-start(f32[64]{0:T(128)} %param.9) | copy-start | bytes 772
  5.7 4.3 %copy-start.1 = (bf16[16,16,1,1024]{3,1,2,0:T(8,128)(2,1)S(1)}, bf16[16,16,1,1024]{3,1,2,0:T(8,128)(2,1)}, u32[]{:S(2)}) copy-start(bf16[16,16,1,1024]{3,1,2,0:T(8,128)(2,1)} %param.6) | copy-start | bytes 1572868
  5.7 7.0 %copy-start.2 = (bf16[16,16,1,1024]{3,1,2,0:T(8,128)(2,1)S(1)}, bf16[16,16,1,1024]{3,1,2,0:T(8,128)(2,1)}, u32[]{:S(2)}) copy-start(bf16[16,16,1,1024]{3,1,2,0:T(8,128)(2,1)} %param.11) | copy-start | bytes 1572868
  6.7 5.7 %collective-permute-start.2 = (bf16[18,1024]{1,0:T(8,128)(2,1)S(1)}, bf16[18,1024]{1,0:T(8,128)(2,1)S(1)}, u32[]{:S(2)}, u32[]{:S(2)}) collective-permute-start(bf16[18,1024]{1,0:T(8,128)(2,1)S(1)} %get-tuple-element.56), channel_id=1, source_target_pairs={{0,4},{1,2},{2,1},{3,7},{4,0},{5,6},{6,5},{7,3},{8,12},{9,10},{10,... | collective-permute-start | bytes 110600 | tf_op jit(solution)/shard_map/ppermute | solution.py:363
  7.0 5.7 %collective-permute-start.3 = (bf16[18,1024]{1,0:T(8,128)(2,1)S(1)}, bf16[18,1024]{1,0:T(8,128)(2,1)S(1)}, u32[]{:S(2)}, u32[]{:S(2)}) collective-permute-start(bf16[18,1024]{1,0:T(8,128)(2,1)S(1)} %get-tuple-element.57), channel_id=1, source_target_pairs={{0,1},{1,0},{2,3},{3,2},{4,5},{5,4},{6,7},{7,6},{8,9},{9,8},{10,11... | collective-permute-start | bytes 110600 | tf_op jit(solution)/shard_map/ppermute | solution.py:364
  15.1 4.8 %collective-permute-start.5 = (bf16[16,1024]{1,0:T(8,128)(2,1)S(1)}, bf16[16,1024]{1,0:T(8,128)(2,1)S(1)}, u32[]{:S(2)}, u32[]{:S(2)}) collective-permute-start(bf16[16,1024]{1,0:T(8,128)(2,1)S(1)} %get-tuple-element.65), channel_id=1, source_target_pairs={{0,1},{1,0},{2,3},{3,2},{4,8},{5,9},{6,10},{7,11},{8,4},{9,5},{10,... | collective-permute-start | bytes 98312 | tf_op jit(solution)/shard_map/ppermute | solution.py:363
  16.5 3.4 %collective-permute-start.6 = (bf16[16,1024]{1,0:T(8,128)(2,1)S(1)}, bf16[16,1024]{1,0:T(8,128)(2,1)S(1)}, u32[]{:S(2)}, u32[]{:S(2)}) collective-permute-start(bf16[16,1024]{1,0:T(8,128)(2,1)S(1)} %get-tuple-element.66), channel_id=1, source_target_pairs={{0,4},{4,0},{8,12},{12,8},{16,20},{20,16},{24,28},{28,24},{1,5},{5... | collective-permute-start | bytes 98312 | tf_op jit(solution)/shard_map/ppermute | solution.py:364
  18.5 1.4 %collective-permute-start.4 = (f32[48,128]{1,0:T(8,128)S(1)}, f32[48,128]{1,0:T(8,128)S(1)}, u32[]{:S(2)}, u32[]{:S(2)}) collective-permute-start(f32[48,128]{1,0:T(8,128)S(1)} %sums.1), channel_id=1, source_target_pairs={{0,4},{4,0},{8,12},{12,8},{16,20},{20,16},{24,28},{28,24},{1,5},{5... | collective-permute-start | bytes 73736 | tf_op jit(solution)/shard_map/ppermute | solution.py:461
  20.0 4.3 %collective-permute-start.7 = (f32[48,128]{1,0:T(8,128)S(1)}, f32[48,128]{1,0:T(8,128)S(1)}, u32[]{:S(2)}, u32[]{:S(2)}) collective-permute-start(f32[48,128]{1,0:T(8,128)S(1)} %add.26), channel_id=1, source_target_pairs={{0,8},{4,12},{8,0},{12,4},{16,24},{20,28},{24,16},{28,20},{1,9},{5... | collective-permute-start | bytes 73736 | tf_op jit(solution)/shard_map/ppermute | solution.py:464
  21.5 8.4 %collective-permute-start.10 = (bf16[18,1024]{1,0:T(8,128)(2,1)S(1)}, bf16[18,1024]{1,0:T(8,128)(2,1)S(1)}, u32[]{:S(2)}, u32[]{:S(2)}) collective-permute-start(bf16[18,1024]{1,0:T(8,128)(2,1)S(1)} %get-tuple-element.78), channel_id=1, source_target_pairs={{0,4},{1,2},{2,1},{3,7},{4,0},{5,6},{6,5},{7,3},{8,12},{9,10},{10,... | collective-permute-start | bytes 110600 | tf_op jit(solution)/shard_map/ppermute | solution.py:363
  21.5 8.4 %collective-permute-start.11 = (bf16[18,1024]{1,0:T(8,128)(2,1)S(1)}, bf16[18,1024]{1,0:T(8,128)(2,1)S(1)}, u32[]{:S(2)}, u32[]{:S(2)}) collective-permute-start(bf16[18,1024]{1,0:T(8,128)(2,1)S(1)} %get-tuple-element.79), channel_id=1, source_target_pairs={{0,1},{1,0},{2,3},{3,2},{4,5},{5,4},{6,7},{7,6},{8,9},{9,8},{10,11... | collective-permute-start | bytes 110600 | tf_op jit(solution)/shard_map/ppermute | solution.py:364
  24.3 4.8 %collective-permute-start.8 = (f32[48,128]{1,0:T(8,128)S(1)}, f32[48,128]{1,0:T(8,128)S(1)}, u32[]{:S(2)}, u32[]{:S(2)}) collective-permute-start(f32[48,128]{1,0:T(8,128)S(1)} %add.27), channel_id=1, source_target_pairs={{0,16},{4,20},{8,24},{12,28},{16,0},{20,4},{24,8},{28,12},{1,17},{... | collective-permute-start | bytes 73736 | tf_op jit(solution)/shard_map/ppermute | solution.py:467
  29.1 3.8 %collective-permute-start.9 = (f32[48,128]{1,0:T(8,128)S(1)}, f32[48,128]{1,0:T(8,128)S(1)}, u32[]{:S(2)}, u32[]{:S(2)}) collective-permute-start(f32[48,128]{1,0:T(8,128)S(1)} %add.28), channel_id=1, source_target_pairs={{0,1},{1,0},{2,3},{3,2},{4,5},{5,4},{6,7},{7,6},{8,9},{9,8},{10,11... | collective-permute-start | bytes 73736 | tf_op jit(solution)/shard_map/ppermute | solution.py:482
  33.0 3.8 %collective-permute-start.12 = (f32[48,128]{1,0:T(8,128)S(1)}, f32[48,128]{1,0:T(8,128)S(1)}, u32[]{:S(2)}, u32[]{:S(2)}) collective-permute-start(f32[48,128]{1,0:T(8,128)S(1)} %add.29.mine_ref), channel_id=1, source_target_pairs={{0,2},{1,3},{2,0},{3,1},{4,6},{5,7},{6,4},{7,5},{8,10},{9,11},{10,... | collective-permute-start | bytes 73736 | tf_op jit(solution)/shard_map/ppermute | solution.py:486

commit v2 on v1

--- a/solution.py
+++ b/solution.py
@@ -126,6 +126,8 @@
         for j, t in enumerate(place(i, ref)):
             field[j, plane * pitch + 8:plane * pitch + 8 + side, :] = t
 
+    totals = []
+
     def x_tile(k):
         for plane, off_x, x in ((0, 0, 0), (side + 1, 2, side - 1)):
             for half in range(side // 8):
@@ -134,15 +136,19 @@
                 for (off_y, off_z), value in shifted(field, tiles, k, plane, half, pitch).items():
                     tap = 9 * off_x + 3 * off_y + off_z
                     total = total + value * weights[26 - tap if flip else tap]
-                sums[k, row:row + 8, :] = total
+                totals.append((k, slice(row, row + 8), total))
 
     for k in range(tiles):
         x_tile(k)
+    for k, at, total in totals:
+        sums[k, at, :] = total
 
     for i, ref, shift in ((2, ylo_ref, 7), (3, yhi_ref, pitch)):
         for j, t in enumerate(place(i, ref)):
             for start, size, at in column_starts(side, shift):
                 field[j, at, :] = t[start:start + size]
+
+    totals = []
 
     def y_tile(k):
         for shift, off_y, y in ((7, 0, 0), (pitch, 2, side - 1)):
@@ -155,10 +161,12 @@
                         tap = 9 * off_x + 3 * off_y + off_z
                         value = field[i, pl.ds((x + off_x) * pitch + shift, 8, stride=pitch), :]
                         total = total + value * weights[26 - tap if flip else tap]
-                sums[k, at, :] = total
+                totals.append((k, at, total))
 
     for k in range(tiles):
         y_tile(k)
+    for k, at, total in totals:
+        sums[k, at, :] = total
 
 
 def shifted(field, tiles, k, plane, half, pitch):
@@ -223,39 +231,29 @@
     mean_mat = mean_mat_ref[...]
     mix_mat = mix_mat_ref[...]
     gain = gain_wide_ref[...]
-    rows = 128
-    xs = rows // side
     gain_sum = jnp.zeros((8, WIDE), F32)
     mix_sum = jnp.zeros((WIDE, WIDE), F32)
     for part in range(lanes // WIDE):
         cols = slice(part * WIDE, (part + 1) * WIDE)
-        for chunk in range(cells // rows):
-            at = slice(chunk * rows, (chunk + 1) * rows)
-            planes = slice(chunk * xs, (chunk + 1) * xs)
-            dep = jnp.concatenate([depth[2 * part, at, :], depth[2 * part + 1, at, :]], axis=1)
-            mean_sq = jnp.dot((dep * dep).astype(BF16), mean_mat, preferred_element_type=F32)
-            inv = lax.rsqrt(mean_sq + EPS)
-            normed = dep * inv
-            norm_bf = (normed * gain).astype(BF16)
-            normed_bf[at, cols] = norm_bf
-            grad_norm = lax.dot_general(
-                cot_ref[planes, :, cols].reshape(rows, WIDE), mix_mat,
-                (((1,), (1,)), ((), ())), preferred_element_type=F32,
-            )
-            gain_sum = gain_sum + jnp.sum((grad_norm * normed).reshape(rows // 8, 8, WIDE), axis=0)
-            scaled = grad_norm * gain
-            mean = jnp.dot((scaled * normed).astype(BF16), mean_mat, preferred_element_type=F32)
-            grad = (inv * (scaled - normed * mean)).astype(BF16)
-            grad_ref[planes, :, cols] = grad.reshape(xs, side, WIDE)
-            wide_grad = grad.astype(F32)
-            grads[2 * part, at, :] = wide_grad[:, :LANE]
-            grads[2 * part + 1, at, :] = wide_grad[:, LANE:]
+        dep = jnp.concatenate([depth[2 * part], depth[2 * part + 1]], axis=1)
+        cot = cot_ref[:, :, cols].reshape(cells, WIDE)
+        mean_sq = jnp.dot((dep * dep).astype(BF16), mean_mat, preferred_element_type=F32)
+        grad_norm = lax.dot_general(cot, mix_mat, (((1,), (1,)), ((), ())), preferred_element_type=F32)
+        inv = lax.rsqrt(mean_sq + EPS)
+        normed = dep * inv
+        norm_bf = (normed * gain).astype(BF16)
+        scaled = grad_norm * gain
+        mean = jnp.dot((scaled * normed).astype(BF16), mean_mat, preferred_element_type=F32)
         mix_sum = mix_sum + lax.dot_general(
-            normed_bf[:, cols],
-            cot_ref[:, :, cols].reshape(cells, WIDE),
-            (((0,), (0,)), ((), ())),
-            preferred_element_type=F32,
+            norm_bf, cot, (((0,), (0,)), ((), ())), preferred_element_type=F32
         )
+        gain_sum = gain_sum + jnp.sum((grad_norm * normed).reshape(cells // 8, 8, WIDE), axis=0)
+        grad = (inv * (scaled - normed * mean)).astype(BF16)
+        wide_grad = grad.astype(F32)
+        normed_bf[:, cols] = norm_bf
+        grad_ref[:, :, cols] = grad.reshape(side, side, WIDE)
+        grads[2 * part] = wide_grad[:, :LANE]
+        grads[2 * part + 1] = wide_grad[:, LANE:]
     gain_sum_ref[...] = gain_sum
     channels = grad_mix_ref.shape[1] // 2
     grad_mix = mix_sum[:channels, :channels]

time: 37.8 us -> 37.2 us (0.984)
  Pallas kernels: 12.9 us -> 12.3 us
    pallas_call x10, Pallas kernels: 12.9 us -> 12.3 us  [call(): pl.pallas_call(kernel, out_shape=tuple((jax.ShapeDtypeStruct(t.shape, t.d...]
  transfers between devices with their start and end apart: 13 -> 13, of which waited for: 5 -> 5; matrix products, arithmetic and copies ran while one was open for 0% -> 0% of each run, Pallas kernels for 26% -> 27%
where the time goes in v2:
time: 37.2 us; the launch traced here: 36.9 us
  starting transfers between devices  15.9 us (43%)
  Pallas kernels  12.3 us (33%)
  waiting for transfers between devices  5.42 us (15%)
  local copies, waits for them, and re-layouts  1.62 us (4%)
  other arithmetic  0.96 us (3%)
  between operations  0.8 us (2%)
    pallas_call x10, Pallas kernels, call(): pl.pallas_call(kernel, out_shape=tuple((jax.ShapeDtypeStruct(t.shape, t.d...  12.3 us
    ppermute x4, starting transfers between devices, swap(): lax.ppermute(to_first, axis, [(i, i ^ 1) for i in range(count)])  6 us
    ppermute x4, starting transfers between devices, swap(): lax.ppermute(to_second, ('gx', 'gy'), [(index(p), index(second(p))) for p...  4.79 us
    ppermute x1, waiting for transfers between devices, shards(): theirs = lax.ppermute(part, *steps[-1])  1.99 us
    ppermute x1, starting transfers between devices, shards(): theirs = lax.ppermute(part, *steps[2])  1.61 us
    ppermute x1, waiting for transfers between devices, shards(): part = part + lax.ppermute(part, *step)  1.6 us
    unnamed x14, local copies, waits for them, and re-layouts  1.58 us
    ppermute x1, starting transfers between devices, shards(): part = part + lax.ppermute(part, *steps[1])  1.48 us
  transfers between devices with their start and end apart: 13, of which 5 were waited for; matrix products, arithmetic and copies ran while one was open for 0% of the time, Pallas kernels for 27%

profile of v2, /device:TPU:0, one launch (start us, length us, event | category | flops | bytes accessed | tf_op | source)
XLA Modules:
  0.0 36.9 jit_solution(6673753715498097268)
XLA Ops:
  0.6 0.8 %select_bitcast_fusion.1 = (bf16[16,1024]{1,0:T(8,128)(2,1)S(1)}, bf16[16,1024]{1,0:T(8,128)(2,1)S(1)}) fusion(pred[]{:T(512)S(6)} %eq.23, bf16[16,16,1,1024]{3,1,2,0:T(8,128)(2,1)} %param.6), kind=kLoop, calls=%fused_computation.13 | loop fusion | flops 32768 | bytes 131073 | tf_op jit(solution)/shard_map/jit(_where)/select_n | solution.py:184
  1.4 3.0 %collective-permute-start = (bf16[16,1024]{1,0:T(8,128)(2,1)S(1)}, bf16[16,1024]{1,0:T(8,128)(2,1)S(1)}, u32[]{:S(2)}, u32[]{:S(2)}) collective-permute-start(bf16[16,1024]{1,0:T(8,128)(2,1)S(1)} %get-tuple-element.94), channel_id=1, source_target_pairs={{0,1},{1,0},{2,3},{3,2},{4,8},{5,9},{6,10},{7,11},{8,4},{9,5},{10,... | collective-permute-start | bytes 98312 | tf_op jit(solution)/shard_map/ppermute | solution.py:361
  4.4 0.2 collective-permute-start.1
  4.6 1.0 %copy-done = bf16[16,16,1,1024]{3,1,2,0:T(8,128)(2,1)S(1)} copy-done((bf16[16,16,1,1024]{3,1,2,0:T(8,128)(2,1)S(1)}, bf16[16,16,1,1024]{3,1,2,0:T(8,128)(2,1)}, u32[]{:S(2)}) %copy-start) | copy-done | bytes 524312
  5.7 0.0 copy-start.1
  5.7 0.0 copy-start.2
  5.7 0.2 y_edges.1
  5.9 0.5 %copy-done.3 = bf16[64,64]{1,0:T(8,128)(2,1)S(1)} copy-done((bf16[64,64]{1,0:T(8,128)(2,1)S(1)}, bf16[64,64]{1,0:T(8,128)(2,1)}, u32[]{:S(2)}) %copy-start.3) | copy-done | bytes 8216
  6.4 0.0 copy-done.4
  6.4 0.0 copy-done.5
  6.4 0.0 copy-done.6
  6.4 0.1 params.1
  6.5 0.0 collective-permute-done
  6.6 0.0 collective-permute-done.1
  6.6 0.1 broadcast_select_fusion.6
  6.7 0.4 %collective-permute-start.2 = (bf16[18,1024]{1,0:T(8,128)(2,1)S(1)}, bf16[18,1024]{1,0:T(8,128)(2,1)S(1)}, u32[]{:S(2)}, u32[]{:S(2)}) collective-permute-start(bf16[18,1024]{1,0:T(8,128)(2,1)S(1)} %get-tuple-element.56), channel_id=1, source_target_pairs={{0,4},{1,2},{2,1},{3,7},{4,0},{5,6},{6,5},{7,3},{8,12},{9,10},{10,... | collective-permute-start | bytes 110600 | tf_op jit(solution)/shard_map/ppermute | solution.py:361
  7.0 3.0 %collective-permute-start.3 = (bf16[18,1024]{1,0:T(8,128)(2,1)S(1)}, bf16[18,1024]{1,0:T(8,128)(2,1)S(1)}, u32[]{:S(2)}, u32[]{:S(2)}) collective-permute-start(bf16[18,1024]{1,0:T(8,128)(2,1)S(1)} %get-tuple-element.57), channel_id=1, source_target_pairs={{0,1},{1,0},{2,3},{3,2},{4,5},{5,4},{6,7},{7,6},{8,9},{9,8},{10,11... | collective-permute-start | bytes 110600 | tf_op jit(solution)/shard_map/ppermute | solution.py:362
  10.0 0.0 copy-done.1
  10.0 2.4 %own_forward.1 = (f32[17,440,128]{2,1,0:T(8,128)S(1)}, f32[8,256,128]{2,1,0:T(8,128)S(1)}) custom-call(bf16[16,16,1024]{2,1,0:T(8,128)(2,1)S(1)} %bitcast.16, f32[27,8,128]{2,1,0:T(8,128)S(1)} %get-tuple-element.50.weights), custom_call_target="tpu_custom_call" | custom-call | flops 10000000 | bytes 500000 | tf_op jit(solution)/shard_map/own_forward/pallas_call | solution.py:403
  12.4 0.0 collective-permute-done.2
  12.4 0.3 collective-permute-done.3
  12.7 0.0 copy-done.2
  12.7 1.8 %forward.1 = (f32[17,440,128]{2,1,0:T(8,128)S(1)}, f32[8,256,128]{2,1,0:T(8,128)S(1)}, bf16[16,16,1024]{2,1,0:T(8,128)(2,1)S(1)}, bf16[16,1024]{1,0:T(8,128)(2,1...) custom-call(f32[17,440,128]{2,1,0:T(8,128)S(1)} %get-tuple-element.5, ...), custom_call_target="tpu_custom_call", output_to_operand_aliasing={{0}: (0, {}), {1}: (1, {})} | custom-call | flops 10000000 | bytes 500000 | tf_op jit(solution)/shard_map/forward/pallas_call | solution.py:403
  14.5 1.4 %collective-permute-start.5 = (bf16[16,1024]{1,0:T(8,128)(2,1)S(1)}, bf16[16,1024]{1,0:T(8,128)(2,1)S(1)}, u32[]{:S(2)}, u32[]{:S(2)}) collective-permute-start(bf16[16,1024]{1,0:T(8,128)(2,1)S(1)} %get-tuple-element.65), channel_id=1, source_target_pairs={{0,1},{1,0},{2,3},{3,2},{4,8},{5,9},{6,10},{7,11},{8,4},{9,5},{10,... | collective-permute-start | bytes 98312 | tf_op jit(solution)/shard_map/ppermute | solution.py:361
  15.9 0.0 collective-permute-start.6
  15.9 2.0 %sums.1 = f32[48,128]{1,0:T(8,128)S(1)} custom-call(f32[17,440,128]{2,1,0:T(8,128)S(1)} %get-tuple-element.59.field, f32[8,256,128]{2,1,0:T(8,128)S(1)} %get-tuple-element.60.grads, f32[8,256]{1,0:T(8,128)S(1)} %get-tuple-element.61.gain_sum_ref, f32[32,128]{1,0:T(8,128)S(1)} %get-tuple-element.62.grad_mix_ref), custom_call_target="tpu_custom_call" | custom-call | flops 10000000 | bytes 500000 | tf_op jit(solution)/shard_map/sums/pallas_call | solution.py:403
  17.9 0.5 %collective-permute-start.4 = (f32[48,128]{1,0:T(8,128)S(1)}, f32[48,128]{1,0:T(8,128)S(1)}, u32[]{:S(2)}, u32[]{:S(2)}) collective-permute-start(f32[48,128]{1,0:T(8,128)S(1)} %sums.1), channel_id=1, source_target_pairs={{0,4},{4,0},{8,12},{12,8},{16,20},{20,16},{24,28},{28,24},{1,5},{5... | collective-permute-start | bytes 73736 | tf_op jit(solution)/shard_map/ppermute | solution.py:459
  18.4 0.2 grad_y_edges.1
  18.6 0.7 %collective-permute-done.4 = f32[48,128]{1,0:T(8,128)S(1)} collective-permute-done((f32[48,128]{1,0:T(8,128)S(1)}, f32[48,128]{1,0:T(8,128)S(1)}, u32[]{:S(2)}, u32[]{:S(2)}) %collective-permute-start.4) | collective-permute-done | bytes 24608 | tf_op jit(solution)/shard_map/ppermute | solution.py:459
  19.3 0.0 collective-permute-done.5
  19.3 0.0 collective-permute-done.6
  19.4 0.1 broadcast_select_fusion.2
  19.4 1.5 %collective-permute-start.7 = (f32[48,128]{1,0:T(8,128)S(1)}, f32[48,128]{1,0:T(8,128)S(1)}, u32[]{:S(2)}, u32[]{:S(2)}) collective-permute-start(f32[48,128]{1,0:T(8,128)S(1)} %add.26), channel_id=1, source_target_pairs={{0,8},{4,12},{8,0},{12,4},{16,24},{20,28},{24,16},{28,20},{1,9},{5... | collective-permute-start | bytes 73736 | tf_op jit(solution)/shard_map/ppermute | solution.py:462
  20.9 0.0 collective-permute-start.10
  20.9 2.8 %collective-permute-start.11 = (bf16[18,1024]{1,0:T(8,128)(2,1)S(1)}, bf16[18,1024]{1,0:T(8,128)(2,1)S(1)}, u32[]{:S(2)}, u32[]{:S(2)}) collective-permute-start(bf16[18,1024]{1,0:T(8,128)(2,1)S(1)} %get-tuple-element.79), channel_id=1, source_target_pairs={{0,1},{1,0},{2,3},{3,2},{4,5},{5,4},{6,7},{7,6},{8,9},{9,8},{10,11... | collective-permute-start | bytes 110600 | tf_op jit(solution)/shard_map/ppermute | solution.py:362
  23.8 0.0 collective-permute-done.7
  23.8 1.6 %collective-permute-start.8 = (f32[48,128]{1,0:T(8,128)S(1)}, f32[48,128]{1,0:T(8,128)S(1)}, u32[]{:S(2)}, u32[]{:S(2)}) collective-permute-start(f32[48,128]{1,0:T(8,128)S(1)} %add.27), channel_id=1, source_target_pairs={{0,16},{4,20},{8,24},{12,28},{16,0},{20,4},{24,8},{28,12},{1,17},{... | collective-permute-start | bytes 73736 | tf_op jit(solution)/shard_map/ppermute | solution.py:465
  25.4 2.4 %own_backward.1 = (f32[17,440,128]{2,1,0:T(8,128)S(1)}, f32[8,256,128]{2,1,0:T(8,128)S(1)}) custom-call(bf16[16,16,1024]{2,1,0:T(8,128)(2,1)S(1)} %get-tuple-element.72.cells_ref.own_ref, f32[27,8,128]{2,1,0:T(8,128)S(1)} %get-tuple-element.50.weights), custom_call_target="tpu_custom_call" | custom-call | flops 10000000 | bytes 500000 | tf_op jit(solution)/shard_map/own_backward/pallas_call | solution.py:403
  27.7 0.8 %collective-permute-done.8 = f32[48,128]{1,0:T(8,128)S(1)} collective-permute-done((f32[48,128]{1,0:T(8,128)S(1)}, f32[48,128]{1,0:T(8,128)S(1)}, u32[]{:S(2)}, u32[]{:S(2)}) %collective-permute-start.8) | collective-permute-done | bytes 24608 | tf_op jit(solution)/shard_map/ppermute | solution.py:465
  28.6 0.8 %collective-permute-start.9 = (f32[48,128]{1,0:T(8,128)S(1)}, f32[48,128]{1,0:T(8,128)S(1)}, u32[]{:S(2)}, u32[]{:S(2)}) collective-permute-start(f32[48,128]{1,0:T(8,128)S(1)} %add.28), channel_id=1, source_target_pairs={{0,1},{1,0},{2,3},{3,2},{4,5},{5,4},{6,7},{7,6},{8,9},{9,8},{10,11... | collective-permute-start | bytes 73736 | tf_op jit(solution)/shard_map/ppermute | solution.py:480
  29.3 0.0 collective-permute-done.10
  29.3 0.0 collective-permute-done.11
  29.3 1.4 %backward.1 = (f32[17,440,128]{2,1,0:T(8,128)S(1)}, f32[8,256,128]{2,1,0:T(8,128)S(1)}, bf16[16,16,1024]{2,1,0:T(8,128)(2,1)}) custom-call(f32[17,440,128]{2,1,0:T(8,128)S(1)} %get-tuple-element.76.field, f32[8,256,128]{2,1,0:T(8,128)S(1)} %get-tuple-element.77.sums, ...), custom_call_target="tpu_custom_call", output_to_operand_aliasing={{0}: (0, {}), {1}: (1, {})} | custom-call | flops 2000000 | bytes 500000 | tf_op jit(solution)/shard_map/backward/pallas_call | solution.py:403
  30.8 1.6 %collective-permute-done.9 = f32[48,128]{1,0:T(8,128)S(1)} collective-permute-done((f32[48,128]{1,0:T(8,128)S(1)}, f32[48,128]{1,0:T(8,128)S(1)}, u32[]{:S(2)}, u32[]{:S(2)}) %collective-permute-start.9) | collective-permute-done | bytes 24608 | tf_op jit(solution)/shard_map/ppermute | solution.py:480
  32.4 0.7 %collective-permute-start.12 = (f32[48,128]{1,0:T(8,128)S(1)}, f32[48,128]{1,0:T(8,128)S(1)}, u32[]{:S(2)}, u32[]{:S(2)}) collective-permute-start(f32[48,128]{1,0:T(8,128)S(1)} %add.29.mine_ref), channel_id=1, source_target_pairs={{0,2},{1,3},{2,0},{3,1},{4,6},{5,7},{6,4},{7,5},{8,10},{9,11},{10,... | collective-permute-start | bytes 73736 | tf_op jit(solution)/shard_map/ppermute | solution.py:484
  33.1 1.1 %mixed.1 = bf16[16,16,1024]{2,1,0:T(8,128)(2,1)} custom-call(bf16[16,16,1024]{2,1,0:T(8,128)(2,1)S(1)} %bitcast.17, bf16[256,1024]{1,0:T(8,128)(2,1)S(1)} %get-tuple-element.83.normed_bf, bf16[256,256]{1,0:T(8,128)(2,1)S(1)} %get-tuple-element.54.mix_mat_ref), custom_call_target="tpu_custom_call" | custom-call | flops 10000000 | bytes 500000 | tf_op jit(solution)/shard_map/mixed/pallas_call | solution.py:403
  34.2 2.0 %collective-permute-done.12.theirs_ref = f32[48,128]{1,0:T(8,128)S(1)} collective-permute-done((f32[48,128]{1,0:T(8,128)S(1)}, f32[48,128]{1,0:T(8,128)S(1)}, u32[]{:S(2)}, u32[]{:S(2)}) %collective-permute-start.12) | collective-permute-done | bytes 24608 | tf_op jit(solution)/shard_map/ppermute | solution.py:484
  36.2 0.7 %unpack.1 = (f32[27,64]{1,0:T(8,128)}, f32[1,64]{1,0:T(1,128)}, f32[64,64]{1,0:T(8,128)}) custom-call(f32[48,128]{1,0:T(8,128)S(1)} %add.29.mine_ref, f32[48,128]{1,0:T(8,128)S(1)} %collective-permute-done.12.theirs_ref), custom_call_target="tpu_custom_call" | custom-call | bytes 500000 | tf_op jit(solution)/shard_map/unpack/pallas_call | solution.py:403
  (16 shorter events, 0.1 us)
Async XLA Ops:
  1.4 5.1 %collective-permute-start = (bf16[16,1024]{1,0:T(8,128)(2,1)S(1)}, bf16[16,1024]{1,0:T(8,128)(2,1)S(1)}, u32[]{:S(2)}, u32[]{:S(2)}) collective-permute-start(bf16[16,1024]{1,0:T(8,128)(2,1)S(1)} %get-tuple-element.94), channel_id=1, source_target_pairs={{0,1},{1,0},{2,3},{3,2},{4,8},{5,9},{6,10},{7,11},{8,4},{9,5},{10,... | collective-permute-start | bytes 98312 | tf_op jit(solution)/shard_map/ppermute | solution.py:361
  4.4 2.1 %collective-permute-start.1 = (bf16[16,1024]{1,0:T(8,128)(2,1)S(1)}, bf16[16,1024]{1,0:T(8,128)(2,1)S(1)}, u32[]{:S(2)}, u32[]{:S(2)}) collective-permute-start(bf16[16,1024]{1,0:T(8,128)(2,1)S(1)} %get-tuple-element.95), channel_id=1, source_target_pairs={{0,4},{4,0},{8,12},{12,8},{16,20},{20,16},{24,28},{28,24},{1,5},{5... | collective-permute-start | bytes 98312 | tf_op jit(solution)/shard_map/ppermute | solution.py:362
  4.6 1.0 %copy-start = (bf16[16,16,1,1024]{3,1,2,0:T(8,128)(2,1)S(1)}, bf16[16,16,1,1024]{3,1,2,0:T(8,128)(2,1)}, u32[]{:S(2)}) copy-start(bf16[16,16,1,1024]{3,1,2,0:T(8,128)(2,1)} %param.6) | copy-start | bytes 1572868
  5.7 0.7 %copy-start.3 = (bf16[64,64]{1,0:T(8,128)(2,1)S(1)}, bf16[64,64]{1,0:T(8,128)(2,1)}, u32[]{:S(2)}) copy-start(bf16[64,64]{1,0:T(8,128)(2,1)} %mix_ref.1) | copy-start | bytes 24580
  5.7 0.7 %copy-start.4 = (f32[27,64]{1,0:T(8,128)S(1)}, f32[27,64]{1,0:T(8,128)}, u32[]{:S(2)}) copy-start(f32[27,64]{1,0:T(8,128)} %taps_ref.1) | copy-start | bytes 20740
  5.7 0.7 %copy-start.5 = (s32[8,4,2]{0,2,1:T(2,128)S(1)}, s32[8,4,2]{0,2,1:T(2,128)}, u32[]{:S(2)}) copy-start(s32[8,4,2]{0,2,1:T(2,128)} %param.7) | copy-start | bytes 772
  5.7 0.7 %copy-start.6 = (f32[64]{0:T(128)S(1)}, f32[64]{0:T(128)}, u32[]{:S(2)}) copy-start(f32[64]{0:T(128)} %param.9) | copy-start | bytes 772
  5.7 4.3 %copy-start.1 = (bf16[16,16,1,1024]{3,1,2,0:T(8,128)(2,1)S(1)}, bf16[16,16,1,1024]{3,1,2,0:T(8,128)(2,1)}, u32[]{:S(2)}) copy-start(bf16[16,16,1,1024]{3,1,2,0:T(8,128)(2,1)} %param.6) | copy-start | bytes 1572868
  5.7 7.0 %copy-start.2 = (bf16[16,16,1,1024]{3,1,2,0:T(8,128)(2,1)S(1)}, bf16[16,16,1,1024]{3,1,2,0:T(8,128)(2,1)}, u32[]{:S(2)}) copy-start(bf16[16,16,1,1024]{3,1,2,0:T(8,128)(2,1)} %param.11) | copy-start | bytes 1572868
  6.7 5.7 %collective-permute-start.2 = (bf16[18,1024]{1,0:T(8,128)(2,1)S(1)}, bf16[18,1024]{1,0:T(8,128)(2,1)S(1)}, u32[]{:S(2)}, u32[]{:S(2)}) collective-permute-start(bf16[18,1024]{1,0:T(8,128)(2,1)S(1)} %get-tuple-element.56), channel_id=1, source_target_pairs={{0,4},{1,2},{2,1},{3,7},{4,0},{5,6},{6,5},{7,3},{8,12},{9,10},{10,... | collective-permute-start | bytes 110600 | tf_op jit(solution)/shard_map/ppermute | solution.py:361
  7.0 5.7 %collective-permute-start.3 = (bf16[18,1024]{1,0:T(8,128)(2,1)S(1)}, bf16[18,1024]{1,0:T(8,128)(2,1)S(1)}, u32[]{:S(2)}, u32[]{:S(2)}) collective-permute-start(bf16[18,1024]{1,0:T(8,128)(2,1)S(1)} %get-tuple-element.57), channel_id=1, source_target_pairs={{0,1},{1,0},{2,3},{3,2},{4,5},{5,4},{6,7},{7,6},{8,9},{9,8},{10,11... | collective-permute-start | bytes 110600 | tf_op jit(solution)/shard_map/ppermute | solution.py:362
  14.5 4.8 %collective-permute-start.5 = (bf16[16,1024]{1,0:T(8,128)(2,1)S(1)}, bf16[16,1024]{1,0:T(8,128)(2,1)S(1)}, u32[]{:S(2)}, u32[]{:S(2)}) collective-permute-start(bf16[16,1024]{1,0:T(8,128)(2,1)S(1)} %get-tuple-element.65), channel_id=1, source_target_pairs={{0,1},{1,0},{2,3},{3,2},{4,8},{5,9},{6,10},{7,11},{8,4},{9,5},{10,... | collective-permute-start | bytes 98312 | tf_op jit(solution)/shard_map/ppermute | solution.py:361
  15.9 3.4 %collective-permute-start.6 = (bf16[16,1024]{1,0:T(8,128)(2,1)S(1)}, bf16[16,1024]{1,0:T(8,128)(2,1)S(1)}, u32[]{:S(2)}, u32[]{:S(2)}) collective-permute-start(bf16[16,1024]{1,0:T(8,128)(2,1)S(1)} %get-tuple-element.66), channel_id=1, source_target_pairs={{0,4},{4,0},{8,12},{12,8},{16,20},{20,16},{24,28},{28,24},{1,5},{5... | collective-permute-start | bytes 98312 | tf_op jit(solution)/shard_map/ppermute | solution.py:362
  17.9 1.4 %collective-permute-start.4 = (f32[48,128]{1,0:T(8,128)S(1)}, f32[48,128]{1,0:T(8,128)S(1)}, u32[]{:S(2)}, u32[]{:S(2)}) collective-permute-start(f32[48,128]{1,0:T(8,128)S(1)} %sums.1), channel_id=1, source_target_pairs={{0,4},{4,0},{8,12},{12,8},{16,20},{20,16},{24,28},{28,24},{1,5},{5... | collective-permute-start | bytes 73736 | tf_op jit(solution)/shard_map/ppermute | solution.py:459
  19.4 4.3 %collective-permute-start.7 = (f32[48,128]{1,0:T(8,128)S(1)}, f32[48,128]{1,0:T(8,128)S(1)}, u32[]{:S(2)}, u32[]{:S(2)}) collective-permute-start(f32[48,128]{1,0:T(8,128)S(1)} %add.26), channel_id=1, source_target_pairs={{0,8},{4,12},{8,0},{12,4},{16,24},{20,28},{24,16},{28,20},{1,9},{5... | collective-permute-start | bytes 73736 | tf_op jit(solution)/shard_map/ppermute | solution.py:462
  20.9 8.4 %collective-permute-start.10 = (bf16[18,1024]{1,0:T(8,128)(2,1)S(1)}, bf16[18,1024]{1,0:T(8,128)(2,1)S(1)}, u32[]{:S(2)}, u32[]{:S(2)}) collective-permute-start(bf16[18,1024]{1,0:T(8,128)(2,1)S(1)} %get-tuple-element.78), channel_id=1, source_target_pairs={{0,4},{1,2},{2,1},{3,7},{4,0},{5,6},{6,5},{7,3},{8,12},{9,10},{10,... | collective-permute-start | bytes 110600 | tf_op jit(solution)/shard_map/ppermute | solution.py:361
  20.9 8.4 %collective-permute-start.11 = (bf16[18,1024]{1,0:T(8,128)(2,1)S(1)}, bf16[18,1024]{1,0:T(8,128)(2,1)S(1)}, u32[]{:S(2)}, u32[]{:S(2)}) collective-permute-start(bf16[18,1024]{1,0:T(8,128)(2,1)S(1)} %get-tuple-element.79), channel_id=1, source_target_pairs={{0,1},{1,0},{2,3},{3,2},{4,5},{5,4},{6,7},{7,6},{8,9},{9,8},{10,11... | collective-permute-start | bytes 110600 | tf_op jit(solution)/shard_map/ppermute | solution.py:362
  23.8 4.8 %collective-permute-start.8 = (f32[48,128]{1,0:T(8,128)S(1)}, f32[48,128]{1,0:T(8,128)S(1)}, u32[]{:S(2)}, u32[]{:S(2)}) collective-permute-start(f32[48,128]{1,0:T(8,128)S(1)} %add.27), channel_id=1, source_target_pairs={{0,16},{4,20},{8,24},{12,28},{16,0},{20,4},{24,8},{28,12},{1,17},{... | collective-permute-start | bytes 73736 | tf_op jit(solution)/shard_map/ppermute | solution.py:465
  28.6 3.8 %collective-permute-start.9 = (f32[48,128]{1,0:T(8,128)S(1)}, f32[48,128]{1,0:T(8,128)S(1)}, u32[]{:S(2)}, u32[]{:S(2)}) collective-permute-start(f32[48,128]{1,0:T(8,128)S(1)} %add.28), channel_id=1, source_target_pairs={{0,1},{1,0},{2,3},{3,2},{4,5},{5,4},{6,7},{7,6},{8,9},{9,8},{10,11... | collective-permute-start | bytes 73736 | tf_op jit(solution)/shard_map/ppermute | solution.py:480
  32.4 3.8 %collective-permute-start.12 = (f32[48,128]{1,0:T(8,128)S(1)}, f32[48,128]{1,0:T(8,128)S(1)}, u32[]{:S(2)}, u32[]{:S(2)}) collective-permute-start(f32[48,128]{1,0:T(8,128)S(1)} %add.29.mine_ref), channel_id=1, source_target_pairs={{0,2},{1,3},{2,0},{3,1},{4,6},{5,7},{6,4},{7,5},{8,10},{9,11},{10,... | collective-permute-start | bytes 73736 | tf_op jit(solution)/shard_map/ppermute | solution.py:484
